TPU v7x, 128 devices: a whole 4x4x4 slice. The times are simulated.
128 devices in a mesh: gx: 8 (over x, core), gy: 16 (over z, y).
Axes of the slice: x: 4, y: 4, z: 4, core: 2. Of those that a mesh axis runs over, the one named last changes fastest.
Arguments:
- density: bfloat16 [64, 1048576], P(None, ('gx', 'gy')), may hold values from -6 to 6
- points: bfloat16 [3, 1048576], P(None, ('gx', 'gy')), may hold values from -4 to 4
- weights: bfloat16 [1048576], P(('gx', 'gy')), may hold values from 0.0099487305 to 0.039794922
- source_basis: bfloat16 [64, 1048576], P(None, ('gx', 'gy')), may hold values from -0.375 to 0.375
- target_basis: bfloat16 [64, 1048576], P(None, ('gx', 'gy')), may hold values from -0.75 to 0.75
- up_transfer: bfloat16 [4096, 4096], P(('gx', 'gy')), may hold values from -0.375 to 0.375
- down_transfer: bfloat16 [4096, 4096], P(('gx', 'gy')), may hold values from -0.75 to 0.75
- couple_leaf: bfloat16 [4096, 8, 4096], P(('gx', 'gy')), may hold values from -0.25 to 0.25
- couple_upper: bfloat16 [1024, 8, 4096], P(('gx', 'gy')), may hold values from -0.25 to 0.25
- owner_leaf: int32 [4096, 8], P(('gx', 'gy')), may hold values from 0 to 127, all different within a row; in each aligned block of 32 rows (0 to 31, 32 to 63, ...) at most 3 rows name the same one
- local_leaf: int32 [4096, 8], P(('gx', 'gy')), may hold values from 0 to 31
- owner_upper: int32 [1024, 8], P(('gx', 'gy')), may hold values from 0 to 127, all different within a row; in each aligned block of 8 rows (0 to 7, 8 to 15, ...) at most 2 rows name the same one
- local_upper: int32 [1024, 8], P(('gx', 'gy')), may hold values from 0 to 7
- near_list: int32 [4096, 9], P(('gx', 'gy')), may hold values from 0 to 4095, as said below
Outputs:
- product: bfloat16 [64, 1048576], P(None, ('gx', 'gy'))
Inputs may be any that keep to these rules, and one draw needn't show every extreme that they name: `owner_leaf`: each leaf's row names 8 different devices; among the leaves of one device no device is named more than 3 times, and some device is named exactly 3 times. `owner_upper`: each upper cluster's row names 8 different devices; among the upper clusters of one device no device is named more than 2 times, and some device is named exactly 2 times. `near_list`: entry 0 of each leaf's row is the leaf itself; the other 8 entries are distinct other leaves at most 32 places from it in the cyclic order of leaves, and in every draw some entries lie exactly 32 places away.
All inputs are finite; a program needn't handle non-finite values.
Results may differ from a plain program's by a relative error of at most 0.005.
The roundings to bfloat16 on the way count: a program that leaves them out, or rounds other values in their place, can miss the bound.
Values may be sent and summed in bfloat16 or wider, within the bound.
No kernel may reach another device: no remote copies, remote signals or barrier semaphores. Data moves between devices by JAX's collectives and lax.ppermute only.
A program may use at most 128 MiB of HBM per device.

v0:
```python
import jax
import jax.numpy as jnp
from jax import lax
from jax.sharding import PartitionSpec as P

SOFTEN = 0.0025


def passed_along(value, axis, steps):
    count = lax.axis_size(axis)
    pairs = [(source, (source + steps) % count) for source in range(count)]
    return lax.ppermute(value, axis, pairs)


def near_kernel(target_points, source_points, source_weights):
    target_points = target_points.astype(jnp.float32)
    source_points = source_points.astype(jnp.float32)
    first_diff = target_points[0][:, None, :, None] - source_points[0][:, :, None, :]
    second_diff = target_points[1][:, None, :, None] - source_points[1][:, :, None, :]
    third_diff = target_points[2][:, None, :, None] - source_points[2][:, :, None, :]
    distance = first_diff * first_diff + second_diff * second_diff + third_diff * third_diff
    scaled = source_weights.astype(jnp.float32)[:, :, None, :] * lax.rsqrt(distance + SOFTEN)
    return scaled.astype(jnp.bfloat16)


def slot_ranks(owner_flat, devices):
    owner_hits = (owner_flat[:, None] == jnp.arange(devices, dtype=jnp.int32)[None, :]).astype(
        jnp.int32
    )
    return jnp.sum(jnp.cumsum(owner_hits, axis=0) * owner_hits, axis=1) - 1


def body(
    density,
    points,
    weights,
    source_basis,
    target_basis,
    up_transfer,
    down_transfer,
    couple_leaf,
    couple_upper,
    owner_leaf,
    local_leaf,
    owner_upper,
    local_upper,
    near_list,
):
    devices = lax.axis_size(("gx", "gy"))
    leaf_dev = owner_leaf.shape[0]
    upper_dev = owner_upper.shape[0]
    vector_count = density.shape[0]
    rank_size = source_basis.shape[0]
    leaf_size = density.shape[1] // leaf_dev
    block_width = vector_count * rank_size
    density_cube = density.reshape(vector_count, leaf_dev, leaf_size)
    leaf_mult = jnp.einsum(
        "ncp,rcp->cnr",
        density_cube,
        source_basis.reshape(rank_size, leaf_dev, leaf_size),
        preferred_element_type=jnp.float32,
    ).astype(jnp.bfloat16)
    up_mats = up_transfer.reshape(upper_dev, 4, rank_size, rank_size)
    upper_mult = jnp.einsum(
        "jcnr,jcrs->jns",
        leaf_mult.reshape(upper_dev, 4, vector_count, rank_size),
        up_mats,
        preferred_element_type=jnp.float32,
    ).astype(jnp.bfloat16)
    table_rows = jnp.concatenate(
        [leaf_mult.reshape(leaf_dev, block_width), upper_mult.reshape(upper_dev, block_width)],
        axis=0,
    )
    cap_leaf = max(2, 3 * leaf_dev * owner_leaf.shape[1] // (2 * devices))
    cap_upper = max(2, 3 * upper_dev * owner_upper.shape[1] // (2 * devices))
    owner_flat = owner_leaf.reshape(-1)
    upper_flat = owner_upper.reshape(-1)
    leaf_slots = slot_ranks(owner_flat, devices)
    upper_slots = slot_ranks(upper_flat, devices) + cap_leaf
    requests = jnp.zeros((devices, cap_leaf + cap_upper), jnp.int32)
    requests = requests.at[owner_flat, leaf_slots].set(local_leaf.reshape(-1))
    requests = requests.at[upper_flat, upper_slots].set(local_upper.reshape(-1) + leaf_dev)
    found_rows = jnp.take(
        table_rows,
        lax.all_to_all(requests, ("gx", "gy"), split_axis=0, concat_axis=0, tiled=True),
        axis=0,
    )
    replies = lax.all_to_all(found_rows, ("gx", "gy"), split_axis=0, concat_axis=0, tiled=True)
    before_rows = passed_along((density, points, weights), ("gx", "gy"), 1)
    following = passed_along((density, points, weights), ("gx", "gy"), -1)
    leaf_source = replies[owner_flat, leaf_slots].reshape(
        leaf_dev, owner_leaf.shape[1], vector_count, rank_size
    )
    upper_source = replies[upper_flat, upper_slots].reshape(
        upper_dev, owner_upper.shape[1], vector_count, rank_size
    )
    upper_local = jnp.einsum(
        "cknr,ckrs->cns",
        upper_source,
        couple_upper.reshape(upper_dev, owner_upper.shape[1], rank_size, rank_size),
        preferred_element_type=jnp.float32,
    ).astype(jnp.bfloat16)
    handed = jnp.einsum(
        "jns,jcsr->jcnr",
        upper_local,
        down_transfer.reshape(upper_dev, 4, rank_size, rank_size),
        preferred_element_type=jnp.float32,
    ).reshape(leaf_dev, vector_count, rank_size)
    leaf_far = jnp.einsum(
        "cknr,ckrs->cns",
        leaf_source,
        couple_leaf.reshape(leaf_dev, owner_leaf.shape[1], rank_size, rank_size),
        preferred_element_type=jnp.float32,
    )
    leaf_local = (leaf_far + handed).astype(jnp.bfloat16)
    far_field = jnp.einsum(
        "cnr,rcp->ncp",
        leaf_local,
        target_basis.reshape(rank_size, leaf_dev, leaf_size),
        preferred_element_type=jnp.float32,
    )
    window_density = jnp.concatenate([before_rows[0], density, following[0]], axis=1).reshape(
        vector_count, 3 * leaf_dev, leaf_size
    )
    window_points = jnp.concatenate([before_rows[1], points, following[1]], axis=1).reshape(
        3, 3 * leaf_dev, leaf_size
    )
    window_weights = jnp.concatenate([before_rows[2], weights, following[2]], axis=0).reshape(
        3 * leaf_dev, leaf_size
    )
    total_leaves = leaf_dev * devices
    offsets = (near_list - lax.axis_index(("gx", "gy")) * leaf_dev + leaf_dev) % total_leaves
    own_points = points.reshape(3, leaf_dev, leaf_size)
    group_size = min(8, leaf_dev)
    group_count = leaf_dev // group_size

    def near_group(first_row):
        picked = lax.dynamic_slice_in_dim(offsets, first_row, group_size, 0)
        target_points = lax.dynamic_slice_in_dim(own_points, first_row, group_size, 1)
        kernel = near_kernel(
            target_points,
            jnp.take(window_points, picked, axis=1),
            jnp.take(window_weights, picked, axis=0),
        )
        source_density = jnp.take(window_density, picked, axis=1)
        return jnp.einsum(
            "gkpq,ngkq->ngp", kernel, source_density, preferred_element_type=jnp.float32
        )

    near_parts = lax.map(near_group, jnp.arange(group_count, dtype=jnp.int32) * group_size)
    near_field = near_parts.transpose(1, 0, 2, 3).reshape(vector_count, leaf_dev, leaf_size)
    return (far_field + near_field).reshape(vector_count, leaf_dev * leaf_size).astype(jnp.bfloat16)


def solution(mesh):
    placed = (
        P(None, ("gx", "gy")),
        P(None, ("gx", "gy")),
        P(("gx", "gy")),
        P(None, ("gx", "gy")),
        P(None, ("gx", "gy")),
        P(("gx", "gy"), None),
        P(("gx", "gy"), None),
        P(("gx", "gy"), None, None),
        P(("gx", "gy"), None, None),
        P(("gx", "gy"), None),
        P(("gx", "gy"), None),
        P(("gx", "gy"), None),
        P(("gx", "gy"), None),
        P(("gx", "gy"), None),
    )
    return jax.shard_map(
        body, mesh=mesh, in_specs=placed, out_specs=P(None, ("gx", "gy")), check_vma=False
    )
```

profile of v0, /device:TPU:22, one launch (start us, length us, event | category | flops | bytes accessed | tf_op | source)
XLA Modules:
  0.0 297.1 jit_solution(7422814122606156408)
XLA Ops:
  0.0 1.4 collective-permute-start
  1.4 0.7 collective-permute-start.1
  2.1 1.3 collective-permute-start.2
  3.4 0.7 collective-permute-start.3
  4.1 0.8 copy.60
  5.2 0.8 eq.50
  5.9 0.8 reshape.237
  7.3 0.8 copy.65
  9.9 11.0 %scatter_fusion = s32[128,5]{0,1:T(8,128)S(1)} fusion(s32[128,5]{0,1:T(8,128)S(1)} %broadcast_in_dim.65, s32[256]{0:T(256)S(1)} %bitcast.176, s32[256]{0:T(256)S(1)} %reshape.301), kind=kCustom, calls=%fused_computation.6 | custom fusion | bytes 5120 | tf_op jit(solution)/shard_map/scatter | solution.py:81
  21.0 3.4 %scatter_fusion.1 = s32[128,5]{0,1:T(8,128)S(1)} fusion(s32[128,5]{0,1:T(8,128)S(1)} %scatter_fusion, s32[64]{0:T(128)S(1)} %get-tuple-element.82, s32[64]{0:T(128)S(1)} %reshape.307), kind=kCustom, calls=%fused_computation.7 | custom fusion | bytes 1280 | tf_op jit(solution)/shard_map/scatter | solution.py:82
  24.4 0.7 copy.66
  25.2 15.1 %all-to-all-start = ((s32[128,1,5]{2,1,0:T(1,128)}), s32[128,1,5]{2,1,0:T(1,128)S(1)}, u32[]{:S(2)}, u32[]{:S(2)}) async-start(s32[128,1,5]{2,1,0:T(1,128)} %copy.66), calls=%async_computation | async-start | bytes 131072 | tf_op jit(solution)/shard_map/all_to_all | solution.py:85
  40.3 1.3 collective-permute-start.4
  42.1 1.6 convolution_convert_fusion
  44.9 2.1 reshape.247
  47.0 1.3 reshape.248
  48.4 6.9 %reshape.245 = bf16[32,8,64,64]{3,2,1,0:T(8,128)(2,1)} reshape(bf16[32,8,4096]{2,1,0:T(8,128)(2,1)} %param.23) | data formatting | bytes 4194304 | tf_op jit(solution)/shard_map/reshape | solution.py:112
  55.5 5.4 %gather_fusion.3 = bf16[640,4096]{1,0:T(8,128)(2,1)} fusion(bf16[40,4096]{1,0:T(8,128)(2,1)S(1)} %pad_maximum_fusion.1, s32[1024]{0:T(1024)S(1)} %pad_clamp_fusion.1), kind=kCustom, calls=%fused_computation.3 | custom fusion | bytes 10488320 | tf_op jit(solution)/shard_map/jit(_take)/gather | solution.py:83
  60.9 8.4 %reshape.280 = bf16[128,5,4096]{2,1,0:T(8,128)(2,1)} reshape(bf16[640,4096]{1,0:T(8,128)(2,1)} %gather_fusion.3) | data formatting | bytes 10485760 | tf_op jit(solution)/shard_map/jit(_take)/gather | solution.py:83
  69.4 7.6 %broadcast_select_fusion = bf16[128,5,4096]{2,1,0:T(8,128)(2,1)} fusion(bf16[128,5,4096]{2,1,0:T(8,128)(2,1)} %reshape.280, pred[128,5]{1,0:T(8,128)(4,1)S(1)} %copy.68), kind=kLoop, calls=%fused_computation.30 | loop fusion | flops 2621440 | bytes 10486400 | tf_op jit(solution)/shard_map/jit(_take)/select_n | solution.py:83
  77.0 10.2 %all-to-all-start.1 = ((bf16[128,5,4096]{2,1,0:T(8,128)(2,1)}), bf16[128,5,4096]{2,1,0:T(8,128)(2,1)}, u32[]{:S(2)}, u32[]{:S(2)}) async-start(bf16[128,5,4096]{2,1,0:T(8,128)(2,1)} %broadcast_select_fusion), calls=%async_computation.1 | async-start | bytes 16777216 | tf_op jit(solution)/shard_map/all_to_all | solution.py:88
  87.9 0.7 concatenate.31
  88.6 0.7 concatenate.33
  89.4 103.1 %collective-permute-done.5 = bf16[3,8192]{1,0:T(4,128)(2,1)S(1)} collective-permute-done((bf16[3,8192]{1,0:T(4,128)(2,1)S(1)}, bf16[3,8192]{1,0:T(4,128)(2,1)S(1)}, u32[]{:S(2)}, u32[]{:S(2)}) %collective-permute-start.5) | collective-permute-done | bytes 49184 | tf_op jit(solution)/shard_map/ppermute | solution.py:12
  192.6 1.7 pad_maximum_fusion
  194.2 2.1 copy.109
  196.3 68.2 %while.10 = (s32[]{:T(128)}, f32[4,64,8,256]{3,1,2,0:T(8,128)}, s32[4]{0:T(128)S(1)}, s32[32,9]{1,0:T(8,128)S(1)}, bf16[64,96,256]{2,0,1:T(8,128)(2,1)}, /*index...) while((s32[]{:T(128)}, f32[4,64,8,256]{3,1,2,0:T(8,128)}, ...), condition=%wide.region_8.9_spmd, body=%wide.region_7.8_spmd.sunk | while | flops 657219008 | bytes 9710787 | solution.py:150
  200.0 0.7 gather_fusion.1
  200.8 2.6 gather_fusion.2
  203.5 9.9 %fusion.51 = f32[4,64,8,256]{3,1,2,0:T(8,128)} fusion(f32[4,64,8,256]{3,1,2,0:T(8,128)} %get-tuple-element.177, s32[]{:T(128)} %get-tuple-element.176, f32[8,9,256]{2,1,0:T(8,128)S(1)} %get-tuple-element.159, f32[8,256]{1,0:T(8,128)S(1)} %get-tuple-element.160, f32[8,9,256]{2,1,0:T(8,128)S(1)} %get-tuple-element.161, ...), kind=kOutput, calls=%fused_computation.14.clone.1 | convolution fusion | flops 657063936 | bytes 3203656 | tf_op jit(solution)/shard_map/while/body/eval_jaxpr/gkpq,ngkq->ngp/dot_general | solution.py:146
  217.0 0.7 gather_fusion.1
  217.9 2.6 gather_fusion.2
  220.5 9.9 %fusion.51 = f32[4,64,8,256]{3,1,2,0:T(8,128)} fusion(f32[4,64,8,256]{3,1,2,0:T(8,128)} %get-tuple-element.177, s32[]{:T(128)} %get-tuple-element.176, f32[8,9,256]{2,1,0:T(8,128)S(1)} %get-tuple-element.159, f32[8,256]{1,0:T(8,128)S(1)} %get-tuple-element.160, f32[8,9,256]{2,1,0:T(8,128)S(1)} %get-tuple-element.161, ...), kind=kOutput, calls=%fused_computation.14.clone.1 | convolution fusion | flops 657063936 | bytes 3203656 | tf_op jit(solution)/shard_map/while/body/eval_jaxpr/gkpq,ngkq->ngp/dot_general | solution.py:146
  233.0 0.7 gather_fusion
  234.1 0.7 gather_fusion.1
  234.9 2.6 gather_fusion.2
  237.6 9.9 %fusion.51 = f32[4,64,8,256]{3,1,2,0:T(8,128)} fusion(f32[4,64,8,256]{3,1,2,0:T(8,128)} %get-tuple-element.177, s32[]{:T(128)} %get-tuple-element.176, f32[8,9,256]{2,1,0:T(8,128)S(1)} %get-tuple-element.159, f32[8,256]{1,0:T(8,128)S(1)} %get-tuple-element.160, f32[8,9,256]{2,1,0:T(8,128)S(1)} %get-tuple-element.161, ...), kind=kOutput, calls=%fused_computation.14.clone.1 | convolution fusion | flops 657063936 | bytes 3203656 | tf_op jit(solution)/shard_map/while/body/eval_jaxpr/gkpq,ngkq->ngp/dot_general | solution.py:146
  251.1 0.7 gather_fusion.1
  251.9 2.6 gather_fusion.2
  254.6 9.9 %fusion.51 = f32[4,64,8,256]{3,1,2,0:T(8,128)} fusion(f32[4,64,8,256]{3,1,2,0:T(8,128)} %get-tuple-element.177, s32[]{:T(128)} %get-tuple-element.176, f32[8,9,256]{2,1,0:T(8,128)S(1)} %get-tuple-element.159, f32[8,256]{1,0:T(8,128)S(1)} %get-tuple-element.160, f32[8,9,256]{2,1,0:T(8,128)S(1)} %get-tuple-element.161, ...), kind=kOutput, calls=%fused_computation.14.clone.1 | convolution fusion | flops 657063936 | bytes 3203656 | tf_op jit(solution)/shard_map/while/body/eval_jaxpr/gkpq,ngkq->ngp/dot_general | solution.py:146
  264.5 9.2 %copy.71 = bf16[128,5,4096]{2,0,1:T(8,128)(2,1)} copy(bf16[128,5,4096]{2,1,0:T(8,128)(2,1)} %all-to-all-done.1) | data formatting | bytes 10485760 | tf_op jit(solution)/shard_map/all_to_all | solution.py:88
  273.7 6.0 %gather_fusion.4 = bf16[256,4096]{1,0:T(8,128)(2,1)S(1)} fusion(bf16[128,5,4096]{2,0,1:T(8,128)(2,1)} %copy.71, s32[256]{0:T(256)S(1)} %bitcast.175), kind=kCustom, calls=%fused_computation.4 | custom fusion | bytes 4196352 | tf_op jit(solution)/shard_map/gather | solution.py:91
  279.6 5.5 %reshape.244 = bf16[32,8,64,64]{3,2,1,0:T(8,128)(2,1)} reshape(bf16[256,4096]{1,0:T(8,128)(2,1)S(1)} %gather_fusion.4) | data formatting | bytes 4194304 | tf_op jit(solution)/shard_map/reshape | solution.py:91
  285.2 2.5 gather_fusion.5
  287.7 1.1 reshape.246
  288.8 1.5 fusion.26
  290.4 5.7 %fusion.14 = bf16[32,8,8,256]{3,2,1,0:T(8,128)(2,1)S(1)} fusion(f32[4,64,8,256]{3,1,2,0:T(8,128)} %get-tuple-element.47, bf16[8,32,8,256]{3,2,1,0:T(8,128)(2,1)} %bitcast.184, f32[32,64,64]{2,1,0:T(8,128)S(1)} %bitcast.179, bf16[32,8,64,64]{3,2,1,0:T(8,128)(2,1)} %reshape.244, bf16[32,8,64,64]{3,2,1,0:T(8,128)(2,1)} %reshape.245), kind=kOutput, calls=%fused_computation.35 | convolution fusion | flops 202637312 | bytes 8912896 | tf_op jit(solution)/shard_map/cnr,rcp->ncp/dot_general | solution.py:116
  296.1 1.0 copy.89
  (118 shorter events, 12.3 us)
Async XLA Ops:
  0.0 42.1 %copy-start.2 = (bf16[64,8192]{1,0:T(8,128)(2,1)S(1)}, bf16[64,8192]{1,0:T(8,128)(2,1)}, u32[]{:S(2)}) copy-start(bf16[64,8192]{1,0:T(8,128)(2,1)} %param.16) | copy-start | bytes 3145732
  0.0 40.2 %copy-start.6 = (bf16[3,8192]{1,0:T(4,128)(2,1)S(1)}, bf16[3,8192]{1,0:T(4,128)(2,1)}, u32[]{:S(2)}) copy-start(bf16[3,8192]{1,0:T(4,128)(2,1)} %param.17) | copy-start | bytes 147460
  0.0 41.6 %copy-start.4 = (bf16[32,4096]{1,0:T(8,128)(2,1)S(1)}, bf16[32,4096]{1,0:T(8,128)(2,1)}, u32[]{:S(2)}) copy-start(bf16[32,4096]{1,0:T(8,128)(2,1)} %param.21) | copy-start | bytes 786436
  0.0 192.5 %collective-permute-start = (bf16[64,8192]{1,0:T(8,128)(2,1)}, bf16[64,8192]{1,0:T(8,128)(2,1)}, u32[]{:S(2)}, u32[]{:S(2)}) collective-permute-start(bf16[64,8192]{1,0:T(8,128)(2,1)} %param.16), channel_id=1, source_target_pairs={{0,1},{1,2},{2,3},{3,4},{4,5},{5,6},{6,7},{7,8},{8,9},{9,10},{10,1... | collective-permute-start | bytes 3145736 | tf_op jit(solution)/shard_map/ppermute | solution.py:12
  1.4 191.2 %collective-permute-start.1 = (bf16[64,8192]{1,0:T(8,128)(2,1)}, bf16[64,8192]{1,0:T(8,128)(2,1)}, u32[]{:S(2)}, u32[]{:S(2)}) collective-permute-start(bf16[64,8192]{1,0:T(8,128)(2,1)} %param.16), channel_id=1, source_target_pairs={{0,127},{1,0},{2,1},{3,2},{4,3},{5,4},{6,5},{7,6},{8,7},{9,8},{10,... | collective-permute-start | bytes 3145736 | tf_op jit(solution)/shard_map/ppermute | solution.py:12
  2.1 85.2 %collective-permute-start.2 = (bf16[8192]{0:T(1024)(128)(2,1)}, bf16[8192]{0:T(1024)(128)(2,1)}, u32[]{:S(2)}, u32[]{:S(2)}) collective-permute-start(bf16[8192]{0:T(1024)(128)(2,1)} %param.18), channel_id=1, source_target_pairs={{0,1},{1,2},{2,3},{3,4},{4,5},{5,6},{6,7},{7,8},{8,9},{9,10},{10,1... | collective-permute-start | bytes 49160 | tf_op jit(solution)/shard_map/ppermute | solution.py:12
  3.4 85.2 %collective-permute-start.3 = (bf16[8192]{0:T(1024)(128)(2,1)}, bf16[8192]{0:T(1024)(128)(2,1)}, u32[]{:S(2)}, u32[]{:S(2)}) collective-permute-start(bf16[8192]{0:T(1024)(128)(2,1)} %param.18), channel_id=1, source_target_pairs={{0,127},{1,0},{2,1},{3,2},{4,3},{5,4},{6,5},{7,6},{8,7},{9,8},{10,... | collective-permute-start | bytes 49160 | tf_op jit(solution)/shard_map/ppermute | solution.py:12
  21.0 23.8 %copy-start.8 = (s32[32,9]{0,1:T(8,128)S(1)}, s32[32,9]{0,1:T(8,128)}, u32[]{:S(2)}) copy-start(s32[32,9]{0,1:T(8,128)} %param.29) | copy-start | bytes 3460
  21.0 23.9 %copy-start.7 = (bf16[8192]{0:T(1024)(128)(2,1)S(1)}, bf16[8192]{0:T(1024)(128)(2,1)}, u32[]{:S(2)}) copy-start(bf16[8192]{0:T(1024)(128)(2,1)} %param.18) | copy-start | bytes 49156
  21.0 23.9 %copy-start.3 = (bf16[8,8,4096]{2,1,0:T(8,128)(2,1)S(1)}, bf16[8,8,4096]{2,1,0:T(8,128)(2,1)}, u32[]{:S(2)}) copy-start(bf16[8,8,4096]{2,1,0:T(8,128)(2,1)} %param.24) | copy-start | bytes 1572868
  25.2 30.1 %all-to-all-start = ((s32[128,1,5]{2,1,0:T(1,128)}), s32[128,1,5]{2,1,0:T(1,128)S(1)}, u32[]{:S(2)}, u32[]{:S(2)}) async-start(s32[128,1,5]{2,1,0:T(1,128)} %copy.66), calls=%async_computation | async-start | bytes 131072 | tf_op jit(solution)/shard_map/all_to_all | solution.py:85
  40.3 6.8 %copy-start.5 = (bf16[32,4096]{1,0:T(8,128)(2,1)S(1)}, bf16[32,4096]{1,0:T(8,128)(2,1)}, u32[]{:S(2)}) copy-start(bf16[32,4096]{1,0:T(8,128)(2,1)} %param.22) | copy-start | bytes 786436
  40.3 49.1 %collective-permute-start.4 = (bf16[3,8192]{1,0:T(4,128)(2,1)S(1)}, bf16[3,8192]{1,0:T(4,128)(2,1)S(1)}, u32[]{:S(2)}, u32[]{:S(2)}) collective-permute-start(bf16[3,8192]{1,0:T(4,128)(2,1)S(1)} %copy-done.6), channel_id=1, source_target_pairs={{0,1},{1,2},{2,3},{3,4},{4,5},{5,6},{6,7},{7,8},{8,9},{9,10},{10,1... | collective-permute-start | bytes 147464 | tf_op jit(solution)/shard_map/ppermute | solution.py:12
  77.0 187.4 %all-to-all-start.1 = ((bf16[128,5,4096]{2,1,0:T(8,128)(2,1)}), bf16[128,5,4096]{2,1,0:T(8,128)(2,1)}, u32[]{:S(2)}, u32[]{:S(2)}) async-start(bf16[128,5,4096]{2,1,0:T(8,128)(2,1)} %broadcast_select_fusion), calls=%async_computation.1 | async-start | bytes 16777216 | tf_op jit(solution)/shard_map/all_to_all | solution.py:88
  87.3 105.2 %collective-permute-start.5 = (bf16[3,8192]{1,0:T(4,128)(2,1)S(1)}, bf16[3,8192]{1,0:T(4,128)(2,1)S(1)}, u32[]{:S(2)}, u32[]{:S(2)}) collective-permute-start(bf16[3,8192]{1,0:T(4,128)(2,1)S(1)} %copy-done.6), channel_id=1, source_target_pairs={{0,127},{1,0},{2,1},{3,2},{4,3},{5,4},{6,5},{7,6},{8,7},{9,8},{10,... | collective-permute-start | bytes 147464 | tf_op jit(solution)/shard_map/ppermute | solution.py:12
  279.6 5.5 %copy-start.1 = (s32[64,1]{0,1:T(1,128)S(1)}, s32[64,1]{0,1:T(1,128)}, u32[]{:S(2)}) copy-start(s32[64,1]{0,1:T(1,128)} %get-tuple-element.83) | copy-start | bytes 772
  285.2 3.7 %copy-start = (bf16[8,8,64,64]{3,2,1,0:T(8,128)(2,1)S(1)}, bf16[8,8,64,64]{3,2,1,0:T(8,128)(2,1)}, u32[]{:S(2)}) copy-start(bf16[8,8,64,64]{3,2,1,0:T(8,128)(2,1)} %reshape.247) | copy-start | bytes 1572868
where the time goes:
time: 298 us; the launch traced here: 297 us
  waiting for transfers between devices  103 us (35%)
  local copies, waits for them, and re-layouts  93.2 us (31%)
  matrix products  48.7 us (16%)
  starting transfers between devices  31.3 us (11%)
  other arithmetic  12.6 us (4%)
  loops' own time  7.77 us (3%)
    ppermute x6, waiting for transfers between devices, passed_along(): return lax.ppermute(value, axis, pairs)  103 us
    dot_general x4, matrix products, near_group(): jnp.einsum('gkpq,ngkq->ngp', kernel, source_density, preferred_element_ty...  39.5 us
    all_to_all x1, starting transfers between devices, body(): lax.all_to_all(requests, ('gx', 'gy'), split_axis=0, concat_axis=0, tiled...  15.1 us
    gather x2, local copies, waits for them, and re-layouts, body(): jnp.take(table_rows, lax.all_to_all(requests, ('gx', 'gy'), split_axis=0,...  13.7 us
    scatter x1, local copies, waits for them, and re-layouts, body(): requests = requests.at[owner_flat, leaf_slots].set(local_leaf.reshape(-1))  11 us
    gather x4, local copies, waits for them, and re-layouts, near_group(): source_density = jnp.take(window_density, picked, axis=1)  10.4 us
    all_to_all x1, starting transfers between devices, body(): lax.all_to_all(found_rows, ('gx', 'gy'), split_axis=0, concat_axis=0, til...  10.2 us
    all_to_all x1, local copies, waits for them, and re-layouts, body(): lax.all_to_all(found_rows, ('gx', 'gy'), split_axis=0, concat_axis=0, til...  9.17 us
  transfers between devices with their start and end apart: 8, of which 1 were waited for; matrix products, arithmetic and copies ran while one was open for 41% of the time, Pallas kernels for 0%

commit v1 on v0

v1 whole, which is shorter than its diff:
```python
import jax
import jax.numpy as jnp
from jax import lax
from jax.experimental import pallas as pl
from jax.experimental.pallas import tpu as pltpu
from jax.sharding import PartitionSpec as P

SOFTEN = 0.0025
AXES = ("gx", "gy")
CAP_LEAF = 3
CAP_UPPER = 2
SLOTS = CAP_LEAF + CAP_UPPER
F32 = jnp.float32
BF16 = jnp.bfloat16
NN = (((1,), (0,)), ((), ()))
NT = (((1,), (1,)), ((), ()))
TN = (((0,), (0,)), ((), ()))
VMEM = pl.BlockSpec(memory_space=pltpu.VMEM)
SMEM = pl.BlockSpec(memory_space=pltpu.SMEM)


def dot(a, b, dims=NN):
    return lax.dot_general(a, b, dims, preferred_element_type=F32)


def passed_along(value, steps):
    count = lax.axis_size(AXES)
    pairs = [(source, (source + steps) % count) for source in range(count)]
    return lax.ppermute(value, AXES, pairs)


def iota(shape, dim):
    return lax.broadcasted_iota(jnp.int32, shape, dim)


def flat_row(table):
    rows, wide = table.shape
    spread = (iota((wide, rows * wide), 1) % wide == iota((wide, rows * wide), 0)).astype(BF16)
    keep = iota((rows, rows * wide), 1) // wide == iota((rows, rows * wide), 0)
    return jnp.sum(
        jnp.where(keep, dot(table.astype(F32).astype(BF16), spread), 0.0), axis=0, keepdims=True
    )


def slots_of(owner, local, first, cap, devices, shift):
    entries = owner.shape[1]
    hit = owner == iota((devices, entries), 0).astype(F32)
    ones = hit.astype(BF16)
    before = (iota((entries, entries), 0) < iota((entries, entries), 1)).astype(BF16)
    rank = jnp.sum(jnp.where(hit, dot(ones, before), 0.0), axis=0, keepdims=True)
    wanted = jnp.where(
        rank + first == iota((8, entries), 0).astype(F32), local + shift, 0.0
    ).astype(BF16)
    return dot(ones, wanted, NT), owner * SLOTS + first + rank


def request_kernel(own_leaf, loc_leaf, own_upper, loc_upper, req_ref, leaf_ref, upper_ref):
    devices = req_ref.shape[0]
    leaf_dev = own_leaf.shape[0]
    req_leaf, at_leaf = slots_of(
        flat_row(own_leaf[...]), flat_row(loc_leaf[...]), 0, CAP_LEAF, devices, 0
    )
    req_upper, at_upper = slots_of(
        flat_row(own_upper[...]), flat_row(loc_upper[...]), CAP_LEAF, CAP_UPPER, devices, leaf_dev
    )
    req_ref[...] = (req_leaf + req_upper).astype(jnp.int32)
    leaf_ref[...] = at_leaf.astype(jnp.int32)
    upper_ref[...] = at_upper.astype(jnp.int32)


def packed(block):
    half = block.shape[0] // 2
    return jnp.concatenate([block[:half], block[half:]], axis=1).astype(BF16)


def multipole_kernel(density, basis, up_ref, table_ref):
    leaf_dev = up_ref.shape[0] // up_ref.shape[1]
    rank = up_ref.shape[1]
    size = density.shape[1] // leaf_dev
    for upper in range(leaf_dev // 4):
        blocks = []
        for leaf in range(4 * upper, 4 * upper + 4):
            cut = slice(leaf * size, (leaf + 1) * size)
            blocks.append(dot(basis[:, cut], density[:, cut], NT).astype(BF16))
            table_ref[leaf] = packed(blocks[-1].astype(F32))
        mats = up_ref[4 * upper * rank : 4 * (upper + 1) * rank]
        total = dot(mats, jnp.concatenate(blocks, axis=0), TN)
        table_ref[leaf_dev + upper] = packed(total)


def serve_kernel(req, table_ref, out_ref):
    per_step = out_ref.shape[0]
    first = pl.program_id(0) * per_step
    half = table_ref.shape[1]
    for t in range(per_step):
        for slot in range(SLOTS):
            row = req[(first + t) * 8 + slot]
            out_ref[t, slot * half : (slot + 1) * half] = table_ref[row]


def pieces(value):
    high = value.astype(BF16).astype(F32)
    middle = (value - high).astype(BF16).astype(F32)
    return high, middle, value - high - middle


def near_kernel(offsets, before, own, following, out_ref, window, scale, rhs, lhs, kern):
    leaves, rows, size = out_ref.shape
    near = offsets.shape[0] // leaves
    one = jnp.ones((3, size), F32)
    zero = jnp.zeros((7, size), F32)
    for place, ref in enumerate((before, own, following)):

        def fill(i, carry, place=place, ref=ref):
            block = ref[:, pl.ds(pl.multiple_of(i * size, size), size)]
            window[place * leaves + i] = block[:rows]
            y = block[rows:].astype(F32)
            scale[place * leaves + i] = y[3:4]
            square = y[0:1] * y[0:1] + y[1:2] * y[1:2] + y[2:3] * y[2:3]
            rhs[place * leaves + i] = jnp.concatenate(
                [-2.0 * y[0:3], one, *pieces(square + SOFTEN), zero], axis=0
            ).astype(BF16)
            if place == 1:
                lhs[i] = jnp.transpose(
                    jnp.concatenate([y[0:3], *pieces(square), one, zero], axis=0)
                ).astype(BF16)
            return carry

        lax.fori_loop(0, leaves, fill, 0)

    def leaf(c, carry):
        for k in range(near):
            w = offsets[c * near + k]
            square = dot(lhs[c], rhs[w])
            kern[k] = (scale[w] * lax.rsqrt(square)).astype(BF16)
        total = jnp.zeros((rows, size), F32)
        for k in range(near):
            total += dot(window[offsets[c * near + k]], kern[k], NT)
        out_ref[c] = total
        return carry

    lax.fori_loop(0, leaves, leaf, 0)


def near_field(offsets, before, own, following, leaves, rows):
    size = own.shape[1] // leaves
    near = offsets.shape[0] // leaves
    return pl.pallas_call(
        near_kernel,
        out_shape=jax.ShapeDtypeStruct((leaves, rows, size), F32),
        in_specs=[SMEM, VMEM, VMEM, VMEM],
        out_specs=VMEM,
        scratch_shapes=[
            pltpu.VMEM((3 * leaves, rows, size), BF16),
            pltpu.VMEM((3 * leaves, 1, size), F32),
            pltpu.VMEM((3 * leaves, 16, size), BF16),
            pltpu.VMEM((leaves, size, 16), BF16),
            pltpu.VMEM((near, size, size), BF16),
        ],
        compiler_params=pltpu.CompilerParams(vmem_limit_bytes=40 << 20),
        cost_estimate=pl.CostEstimate(
            flops=20 * leaves * near * size * size * rows,
            bytes_accessed=6 << 20,
            transcendentals=leaves * near * size * size,
        ),
        name="near",
    )(offsets, before, own, following)


def folded(pair, rank):
    return pair[:rank, :rank] + pair[rank:, rank:]


def final_kernel(at_leaf, at_upper, replies, upper_mats, leaf_mats, down, basis, near, out_ref):
    step = pl.program_id(0)
    rank = down.shape[2]
    vectors, wide = out_ref.shape
    size = wide // 4
    fan = upper_mats.shape[2] // (rank // 2)

    def gathered(places, first):
        return jnp.concatenate([replies[places[first + k]] for k in range(fan)], axis=0)

    upper = folded(dot(upper_mats[0], gathered(at_upper, step * fan)), rank).astype(BF16)
    handed = dot(down[0], upper)
    for child in range(4):
        pair = dot(leaf_mats[child], gathered(at_leaf, (step * 4 + child) * fan))
        local = folded(pair, rank) + handed[child * rank : (child + 1) * rank]
        far = dot(local.astype(BF16), basis[:, child * size : (child + 1) * size], TN)
        out_ref[:, child * size : (child + 1) * size] = (far + near[child]).astype(BF16)


def coupled(mats, rank):
    count, fan = mats.shape[:2]
    cut = mats.reshape(count, fan, 2, rank // 2, rank)
    return cut.transpose(0, 2, 4, 1, 3).reshape(count, 2 * rank, fan * rank // 2)


def body(
    density,
    points,
    weights,
    source_basis,
    target_basis,
    up_transfer,
    down_transfer,
    couple_leaf,
    couple_upper,
    owner_leaf,
    local_leaf,
    owner_upper,
    local_upper,
    near_list,
):
    devices = lax.axis_size(AXES)
    leaves, fan = owner_leaf.shape
    uppers = owner_upper.shape[0]
    vectors = density.shape[0]
    rank = source_basis.shape[0]
    half = rank // 2
    size = density.shape[1] // leaves
    total_leaves = leaves * devices

    requests, at_leaf, at_upper = pl.pallas_call(
        request_kernel,
        out_shape=(
            jax.ShapeDtypeStruct((devices, 8), jnp.int32),
            jax.ShapeDtypeStruct((1, leaves * fan), jnp.int32),
            jax.ShapeDtypeStruct((1, uppers * fan), jnp.int32),
        ),
        in_specs=[VMEM] * 4,
        out_specs=(VMEM, VMEM, VMEM),
        name="requests",
    )(owner_leaf, local_leaf, owner_upper, local_upper)
    asked = lax.all_to_all(requests, AXES, split_axis=0, concat_axis=0, tiled=True)

    own = jnp.concatenate(
        [density, points, weights[None], jnp.zeros((4, density.shape[1]), BF16)], axis=0
    )
    before = passed_along(own, 1)
    following = passed_along(own, -1)

    table = pl.pallas_call(
        multipole_kernel,
        out_shape=jax.ShapeDtypeStruct((leaves + uppers, half, 2 * rank), BF16),
        in_specs=[VMEM] * 3,
        out_specs=VMEM,
        name="multipoles",
    )(density, source_basis, up_transfer.reshape(leaves * rank, rank))

    per_step = 16
    found = pl.pallas_call(
        serve_kernel,
        out_shape=jax.ShapeDtypeStruct((devices, SLOTS * half, 2 * rank), BF16),
        grid_spec=pltpu.PrefetchScalarGridSpec(
            num_scalar_prefetch=1,
            grid=(devices // per_step,),
            in_specs=[pl.BlockSpec(table.shape, lambda i, r: (0, 0, 0))],
            out_specs=pl.BlockSpec((per_step, SLOTS * half, 2 * rank), lambda i, r: (i, 0, 0)),
        ),
        name="serve",
    )(asked.reshape(-1), table)
    replies = lax.all_to_all(found, AXES, split_axis=0, concat_axis=0, tiled=True)

    offsets = (near_list - lax.axis_index(AXES) * leaves + leaves) % total_leaves
    near = near_field(offsets.reshape(-1), before, own, following, leaves, vectors)

    leaf_mats = coupled(couple_leaf, rank)
    upper_mats = coupled(couple_upper, rank)
    down = (
        down_transfer.reshape(uppers, 4, rank, rank)
        .transpose(0, 1, 3, 2)
        .reshape(uppers, 4 * rank, rank)
    )
    whole = (devices * SLOTS, half, 2 * rank)
    return pl.pallas_call(
        final_kernel,
        out_shape=jax.ShapeDtypeStruct(density.shape, BF16),
        grid_spec=pltpu.PrefetchScalarGridSpec(
            num_scalar_prefetch=2,
            grid=(uppers,),
            in_specs=[
                pl.BlockSpec(whole, lambda i, a, b: (0, 0, 0)),
                pl.BlockSpec((1, 2 * rank, fan * half), lambda i, a, b: (i, 0, 0)),
                pl.BlockSpec((4, 2 * rank, fan * half), lambda i, a, b: (i, 0, 0)),
                pl.BlockSpec((1, 4 * rank, rank), lambda i, a, b: (i, 0, 0)),
                pl.BlockSpec((rank, 4 * size), lambda i, a, b: (0, i)),
                pl.BlockSpec((4, vectors, size), lambda i, a, b: (i, 0, 0)),
            ],
            out_specs=pl.BlockSpec((vectors, 4 * size), lambda i, a, b: (0, i)),
        ),
        compiler_params=pltpu.CompilerParams(vmem_limit_bytes=40 << 20),
        name="far",
    )(
        at_leaf.reshape(-1),
        at_upper.reshape(-1),
        replies.reshape(whole),
        upper_mats,
        leaf_mats,
        down,
        target_basis,
        near,
    )


def solution(mesh):
    whole = AXES
    placed = (
        P(None, whole),
        P(None, whole),
        P(whole),
        P(None, whole),
        P(None, whole),
        P(whole, None),
        P(whole, None),
        P(whole, None, None),
        P(whole, None, None),
        P(whole, None),
        P(whole, None),
        P(whole, None),
        P(whole, None),
        P(whole, None),
    )
    return jax.shard_map(
        body, mesh=mesh, in_specs=placed, out_specs=P(None, whole), check_vma=False
    )
```

time: 298 us -> 185 us (0.62)
  the two profiles are of different devices: /device:TPU:22 before, /device:TPU:1 now
where the time goes in v1:
time: 185 us; the launch traced here: 184 us
  Pallas kernels  63.5 us (34%)
  waiting for transfers between devices  49.6 us (27%)
  local copies, waits for them, and re-layouts  44.1 us (24%)
  starting transfers between devices  24.8 us (13%)
  other arithmetic  2.14 us (1%)
    ppermute x2, waiting for transfers between devices, passed_along(): return lax.ppermute(value, AXES, pairs)  46.9 us
    pallas_call x1, Pallas kernels, near_field(): pl.pallas_call(near_kernel, out_shape=jax.ShapeDtypeStruct((leaves, rows,...  35.9 us
    reshape x4, local copies, waits for them, and re-layouts, coupled(): cut = mats.reshape(count, fan, 2, rank // 2, rank)  16.5 us
    pallas_call x1, Pallas kernels, body(): pl.pallas_call(final_kernel, out_shape=jax.ShapeDtypeStruct(density.shape...  16.1 us
    reshape x4, local copies, waits for them, and re-layouts, coupled(): cut.transpose(0, 2, 4, 1, 3).reshape(count, 2 * rank, fan * rank // 2)  13.6 us
    all_to_all x1, starting transfers between devices, body(): lax.all_to_all(requests, AXES, split_axis=0, concat_axis=0, tiled=True)  11.5 us
    all_to_all x1, starting transfers between devices, body(): lax.all_to_all(found, AXES, split_axis=0, concat_axis=0, tiled=True)  7.47 us
    unnamed x24, local copies, waits for them, and re-layouts  6.88 us
  transfers between devices with their start and end apart: 4, of which 2 were waited for; matrix products, arithmetic and copies ran while one was open for 20% of the time, Pallas kernels for 22%

profile of v1, /device:TPU:1, one launch (start us, length us, event | category | flops | bytes accessed | tf_op | source)
XLA Modules:
  0.0 184.3 jit_solution(3531384160096673988)
XLA Ops:
  0.0 1.4 copy.28.own_leaf
  1.4 1.4 copy.29.loc_leaf
  2.7 1.8 requests.1
  4.5 11.5 %all-to-all-start = ((s32[128,1,8]{2,1,0:T(1,128)}), s32[128,1,8]{2,1,0:T(1,128)S(1)}, u32[]{:S(2)}, u32[]{:S(2)}) async-start(s32[128,1,8]{2,1,0:T(1,128)} %bitcast.24), calls=%async_computation | async-start | bytes 131072 | tf_op jit(solution)/shard_map/all_to_all | solution.py:235
  16.0 2.3 %reshape.42.up_ref = bf16[2048,64]{1,0:T(8,128)(2,1)} reshape(bf16[32,4096]{1,0:T(8,128)(2,1)} %param.19) | data formatting | bytes 524288 | tf_op jit(solution)/shard_map/reshape | solution.py:249
  18.3 0.7 broadcast_in_dim.6
  19.1 0.1 pad.3.clone
  19.1 4.0 %multipoles.1.table_ref = bf16[40,32,128]{2,1,0:T(8,128)(2,1)} custom-call(bf16[64,8192]{1,0:T(8,128)(2,1)} %density.1, bf16[64,8192]{1,0:T(8,128)(2,1)} %basis.2, bf16[2048,64]{1,0:T(8,128)(2,1)} %reshape.42.up_ref), custom_call_target="tpu_custom_call" | custom-call | tf_op jit(solution)/shard_map/multipoles/pallas_call | solution.py:243
  23.1 2.7 %all-to-all-done = s32[128,1,8]{2,1,0:T(1,128)S(1)} async-done(((s32[128,1,8]{2,1,0:T(1,128)}), s32[128,1,8]{2,1,0:T(1,128)S(1)}, u32[]{:S(2)}, u32[]{:S(2)}) %all-to-all-start) | async-done | bytes 4128 | tf_op jit(solution)/shard_map/all_to_all | solution.py:235
  25.8 0.5 broadcast.13
  26.3 0.8 reduce.3
  27.1 0.7 reshape.41.req
  27.8 5.7 %serve.1 = bf16[128,160,128]{2,1,0:T(8,128)(2,1)} custom-call(s32[1024]{0:T(1024)} %reshape.41.req, bf16[40,32,128]{2,1,0:T(8,128)(2,1)} %multipoles.1.table_ref), custom_call_target="tpu_custom_call" | custom-call | tf_op jit(solution)/shard_map/serve/pallas_call | solution.py:252
  33.5 7.5 %all-to-all-start.1 = ((bf16[128,160,128]{2,1,0:T(8,128)(2,1)}), bf16[128,160,128]{2,1,0:T(8,128)(2,1)}, u32[]{:S(2)}, u32[]{:S(2)}) async-start(bf16[128,160,128]{2,1,0:T(8,128)(2,1)} %serve.1), calls=%async_computation.1 | async-start | bytes 10485760 | tf_op jit(solution)/shard_map/all_to_all | solution.py:263
  41.0 0.0 copy-done.5
  41.0 0.0 copy-done.9
  41.0 0.0 copy-start.7
  41.1 1.3 maximum_maximum_fusion.own
  42.4 1.4 collective-permute-start
  43.8 4.4 %collective-permute-start.1 = (bf16[72,8192]{1,0:T(8,128)(2,1)}, bf16[72,8192]{1,0:T(8,128)(2,1)}, u32[]{:S(2)}, u32[]{:S(2)}) collective-permute-start(bf16[72,8192]{1,0:T(8,128)(2,1)} %maximum_maximum_fusion.own), channel_id=1, source_target_pairs={{0,127},{1,0},{2,1},{3,2},{4,3},{5,4},{6,5},{7,6},{8,7},{9,8},{10,... | collective-permute-start | bytes 3538952 | tf_op jit(solution)/shard_map/ppermute | solution.py:29
  48.2 0.0 copy-done.7
  48.2 1.1 reshape.44
  49.3 1.1 copy.40
  50.4 0.0 copy-start.6
  50.4 1.3 reshape.45
  51.7 1.2 copy.35.upper_mats
  53.0 0.0 copy-done.6
  53.0 5.5 %reshape.46 = bf16[32,8,2,32,64]{4,3,2,1,0:T(8,128)(2,1)} reshape(bf16[32,8,4096]{2,1,0:T(8,128)(2,1)S(1)} %copy-done.6) | data formatting | bytes 4194304 | tf_op jit(solution)/shard_map/reshape | solution.py:195
  58.5 8.7 %copy.39 = bf16[32,8,2,32,64]{4,2,3,1,0:T(2,128)(2,1)} copy(bf16[32,8,2,32,64]{4,3,2,1,0:T(8,128)(2,1)} %reshape.46) | data formatting | bytes 4194304 | tf_op jit(solution)/shard_map/reshape | solution.py:195
  67.2 7.8 %reshape.47 = bf16[32,128,256]{1,2,0:T(8,128)(2,1)} reshape(bf16[32,2,64,8,32]{2,1,4,3,0:T(2,128)(2,1)} %bitcast.22) | data formatting | bytes 4194304 | tf_op jit(solution)/shard_map/reshape | solution.py:196
  75.0 3.3 %copy.36.leaf_mats = bf16[32,128,256]{2,1,0:T(8,128)(2,1)S(1)} copy(bf16[32,128,256]{1,2,0:T(8,128)(2,1)} %reshape.47) | data formatting | bytes 4194304 | tf_op jit(solution)/shard_map/reshape | solution.py:196
  78.3 0.0 copy-done.8
  78.4 1.3 reshape.48
  79.7 1.3 copy.33
  81.0 0.0 copy-done.10
  81.0 0.1 copy.34
  81.1 0.1 reshape.50.offsets
  81.2 0.0 copy-start.3
  81.2 0.0 copy-start.4
  81.3 46.9 %collective-permute-done.before = bf16[72,8192]{1,0:T(8,128)(2,1)} collective-permute-done((bf16[72,8192]{1,0:T(8,128)(2,1)}, bf16[72,8192]{1,0:T(8,128)(2,1)}, u32[]{:S(2)}, u32[]{:S(2)}) %collective-permute-start) | collective-permute-done | bytes 1179680 | tf_op jit(solution)/shard_map/ppermute | solution.py:29
  128.1 0.0 collective-permute-done.1.following
  128.2 35.9 %near.1 = f32[32,64,256]{2,1,0:T(8,128)S(1)} custom-call(s32[288]{0:T(512)S(1)} %reshape.50.offsets, bf16[72,8192]{1,0:T(8,128)(2,1)} %collective-permute-done.before, bf16[72,8192]{1,0:T(8,128)(2,1)} %maximum_maximum_fusion.own, bf16[72,8192]{1,0:T(8,128)(2,1)} %collective-permute-done.1.following), custom_call_target="tpu_custom_call" | custom-call | flops 24159191040 | bytes 6291456 | tf_op jit(solution)/shard_map/near/pallas_call | solution.py:148
  164.1 0.0 copy-start
  164.1 1.3 copy-done
  165.4 0.0 all-to-all-done.1
  165.4 1.6 copy-done.1
  167.0 1.2 copy-done.2
  168.2 16.1 %far.1 = bf16[64,8192]{1,0:T(8,128)(2,1)} custom-call(s32[256]{0:T(256)S(1)} %bitcast.20, s32[64]{0:T(128)S(1)} %bitcast.21, bf16[640,32,128]{2,1,0:T(8,128)(2,1)} %bitcast.4.replies, bf16[8,128,256]{2,1,0:T(8,128)(2,1)S(1)} %copy.35.upper_mats, bf16[32,128,256]{2,1,0:T(8,128)(2,1)S(1)} %copy.36.leaf_mats, bf16[8,256,64]{2,1,0:T(8,128)(2,1)S(1)} %bitcast.19, ...), custom_call_target="tpu_custom_call" | custom-call | tf_op jit(solution)/shard_map/far/pallas_call | solution.py:276
  (10 shorter events, 0.0 us)
Async XLA Ops:
  4.5 21.3 %all-to-all-start = ((s32[128,1,8]{2,1,0:T(1,128)}), s32[128,1,8]{2,1,0:T(1,128)S(1)}, u32[]{:S(2)}, u32[]{:S(2)}) async-start(s32[128,1,8]{2,1,0:T(1,128)} %bitcast.24), calls=%async_computation | async-start | bytes 131072 | tf_op jit(solution)/shard_map/all_to_all | solution.py:235
  33.5 7.5 %copy-start.5 = (bf16[64,8192]{1,0:T(8,128)(2,1)S(1)}, bf16[64,8192]{1,0:T(8,128)(2,1)}, u32[]{:S(2)}) copy-start(bf16[64,8192]{1,0:T(8,128)(2,1)} %density.1) | copy-start | bytes 3145732
  33.5 7.5 %copy-start.9 = (bf16[3,8192]{1,0:T(4,128)(2,1)S(1)}, bf16[3,8192]{1,0:T(4,128)(2,1)}, u32[]{:S(2)}) copy-start(bf16[3,8192]{1,0:T(4,128)(2,1)} %param.15) | copy-start | bytes 147460
  33.5 131.8 %all-to-all-start.1 = ((bf16[128,160,128]{2,1,0:T(8,128)(2,1)}), bf16[128,160,128]{2,1,0:T(8,128)(2,1)}, u32[]{:S(2)}, u32[]{:S(2)}) async-start(bf16[128,160,128]{2,1,0:T(8,128)(2,1)} %serve.1), calls=%async_computation.1 | async-start | bytes 10485760 | tf_op jit(solution)/shard_map/all_to_all | solution.py:263
  41.0 7.2 %copy-start.7 = (bf16[8,8,4096]{2,1,0:T(8,128)(2,1)S(1)}, bf16[8,8,4096]{2,1,0:T(8,128)(2,1)}, u32[]{:S(2)}) copy-start(bf16[8,8,4096]{2,1,0:T(8,128)(2,1)} %param.22) | copy-start | bytes 1572868
  42.4 85.8 %collective-permute-start = (bf16[72,8192]{1,0:T(8,128)(2,1)}, bf16[72,8192]{1,0:T(8,128)(2,1)}, u32[]{:S(2)}, u32[]{:S(2)}) collective-permute-start(bf16[72,8192]{1,0:T(8,128)(2,1)} %maximum_maximum_fusion.own), channel_id=1, source_target_pairs={{0,1},{1,2},{2,3},{3,4},{4,5},{5,6},{6,7},{7,8},{8,9},{9,10},{10,1... | collective-permute-start | bytes 3538952 | tf_op jit(solution)/shard_map/ppermute | solution.py:29
  43.8 84.4 %collective-permute-start.1 = (bf16[72,8192]{1,0:T(8,128)(2,1)}, bf16[72,8192]{1,0:T(8,128)(2,1)}, u32[]{:S(2)}, u32[]{:S(2)}) collective-permute-start(bf16[72,8192]{1,0:T(8,128)(2,1)} %maximum_maximum_fusion.own), channel_id=1, source_target_pairs={{0,127},{1,0},{2,1},{3,2},{4,3},{5,4},{6,5},{7,6},{8,7},{9,8},{10,... | collective-permute-start | bytes 3538952 | tf_op jit(solution)/shard_map/ppermute | solution.py:29
  50.4 2.6 %copy-start.6 = (bf16[32,8,4096]{2,1,0:T(8,128)(2,1)S(1)}, bf16[32,8,4096]{2,1,0:T(8,128)(2,1)}, u32[]{:S(2)}) copy-start(bf16[32,8,4096]{2,1,0:T(8,128)(2,1)} %param.21) | copy-start | bytes 6291460
  75.0 3.3 %copy-start.8 = (bf16[32,4096]{1,0:T(8,128)(2,1)S(1)}, bf16[32,4096]{1,0:T(8,128)(2,1)}, u32[]{:S(2)}) copy-start(bf16[32,4096]{1,0:T(8,128)(2,1)} %param.20) | copy-start | bytes 786436
  75.0 6.0 %copy-start.10 = (s32[32,9]{0,1:T(8,128)S(1)}, s32[32,9]{0,1:T(8,128)}, u32[]{:S(2)}) copy-start(s32[32,9]{0,1:T(8,128)} %param.27) | copy-start | bytes 3460
  81.2 84.2 %copy-start.3 = (s32[1,256]{1,0:T(1,128)S(1)}, s32[1,256]{1,0:T(1,128)}, u32[]{:S(2)}) copy-start(s32[1,256]{1,0:T(1,128)} %get-tuple-element.8) | copy-start | bytes 3076
  81.2 84.1 %copy-start.4 = (s32[1,64]{1,0:T(1,128)S(1)}, s32[1,64]{1,0:T(1,128)}, u32[]{:S(2)}) copy-start(s32[1,64]{1,0:T(1,128)} %get-tuple-element.9) | copy-start | bytes 772
  164.1 1.3 copy-start
  165.4 1.6 copy-start.1
  167.0 1.2 copy-start.2

commit v2 on v1

v2 whole, which is shorter than its diff:
```python
import jax
import jax.numpy as jnp
from jax import lax
from jax.experimental import pallas as pl
from jax.experimental.pallas import tpu as pltpu
from jax.sharding import PartitionSpec as P

SOFTEN = 0.0025
AXES = ("gx", "gy")
SENT = 56
MOST = 80
F32 = jnp.float32
BF16 = jnp.bfloat16
NN = (((1,), (0,)), ((), ()))
NT = (((1,), (1,)), ((), ()))
TN = (((0,), (0,)), ((), ()))
VMEM = pl.BlockSpec(memory_space=pltpu.VMEM)
SMEM = pl.BlockSpec(memory_space=pltpu.SMEM)


def dot(a, b, dims=NN):
    return lax.dot_general(a, b, dims, preferred_element_type=F32)


def passed_along(value, steps):
    count = lax.axis_size(AXES)
    pairs = [(source, (source + steps) % count) for source in range(count)]
    return lax.ppermute(value, AXES, pairs)


def iota(shape, dim):
    return lax.broadcasted_iota(jnp.int32, shape, dim)


def folded(pair, rank):
    return pair[:rank, :rank] + pair[rank:, rank:]


def flat_row(table):
    wide, rows = table.shape
    spread = (iota((rows, rows * wide), 1) // wide == iota((rows, rows * wide), 0)).astype(BF16)
    keep = iota((wide, rows * wide), 1) % wide == iota((wide, rows * wide), 0)
    return jnp.sum(
        jnp.where(keep, dot(table.astype(F32).astype(BF16), spread), 0.0), axis=0, keepdims=True
    ).astype(jnp.int32)


def request_kernel(own_leaf, loc_leaf, own_upper, loc_upper, ask_ref, place_ref):
    groups = ask_ref.shape[0]
    members = place_ref.shape[0]
    leaves = own_leaf.shape[1]
    owner = jnp.concatenate([flat_row(own_leaf[...]), flat_row(own_upper[...])], axis=1)
    row = jnp.concatenate([flat_row(loc_leaf[...]), flat_row(loc_upper[...]) + leaves], axis=1)
    entries = owner.shape[1]
    group = owner // members
    member = owner - group * members
    hit = group == iota((groups, entries), 0)
    ones = hit.astype(BF16)
    before = (iota((entries, entries), 0) < iota((entries, entries), 1)).astype(BF16)
    rank = jnp.sum(jnp.where(hit, dot(ones, before), 0.0), axis=0, keepdims=True).astype(jnp.int32)
    here = rank == iota((128, entries), 0)
    wanted = [
        dot(ones, jnp.where(here, part.astype(F32), 0.0).astype(BF16), NT) for part in (member, row)
    ]
    most = jnp.max(jnp.sum(hit.astype(F32), axis=1, keepdims=True), axis=0, keepdims=True)
    wanted[0] = jnp.where(iota((groups, 128), 1) == 127, most, wanted[0])
    both = jnp.concatenate(wanted, axis=1)
    for g in range(groups):
        ask_ref[g] = jnp.broadcast_to(both[g : g + 1], ask_ref.shape[1:]).astype(BF16)
    place_ref[...] = jnp.where(iota(place_ref.shape, 0) == 0, group, rank)


def multipole_kernel(density, basis, up_ref, out_ref, square, table, up):
    leaves = up_ref.shape[0]
    rank = square.shape[1]
    half = rank // 2
    rows = table.shape[0] // half
    size = density.shape[1] // leaves
    for leaf in range(leaves):
        cut = slice(leaf * size, (leaf + 1) * size)
        square[leaf * rank : (leaf + 1) * rank] = dot(basis[:, cut], density[:, cut], NT)

    def pack(first, count):
        even = square[pl.ds(first * rank, count * half, stride=2)]
        odd = square[pl.ds(first * rank + 1, count * half, stride=2)]
        table[first * half : (first + count) * half] = jnp.concatenate([even, odd], axis=1)

    pack(0, leaves)
    for j in range(half):
        up[pl.ds(j, leaves, stride=half)] = up_ref[:, j * 2 * rank : (j + 1) * 2 * rank].astype(F32)
    for upper in range(rows - leaves):
        cut = slice(upper * 4 * half, (upper + 1) * 4 * half)
        pair = dot(up[cut].astype(BF16), table[cut].astype(BF16), TN)
        square[(leaves + upper) * rank : (leaves + upper + 1) * rank] = folded(pair, rank)
    pack(leaves, rows - leaves)
    for j in range(half):
        out_ref[j // 2, :, (j % 2) * 2 * rank : (j % 2 + 1) * 2 * rank] = table[
            pl.ds(j, rows, stride=half)
        ].astype(BF16)


def serve_kernel(first, slices, out_ref, codes):
    step = pl.program_id(0)
    members, count, wide = slices.shape
    rows = out_ref.shape[1]
    groups = codes.shape[0]

    @pl.when(step == 0)
    def _():
        asked = slices[:, count - groups :, :].astype(F32)
        code = asked[:, :, : wide // 2] * count + asked[:, :, wide // 2 :]
        for g in range(groups):
            codes[g] = jnp.transpose(code[:, g])

    column = codes[step, first : first + rows]
    lanes = iota((rows, members * count), 1).astype(F32)
    picks = jnp.concatenate(
        [jnp.where(column[:, t : t + 1] == lanes, 1.0, 0.0) for t in range(members)], axis=0
    ).astype(BF16)
    found = dot(picks, slices[...].reshape(members * count, wide))
    out_ref[...] = found.reshape(members, rows, wide).astype(BF16)


def serve(slices, groups, first, rows):
    members, count, wide = slices.shape
    return pl.pallas_call(
        lambda *refs: serve_kernel(first, *refs),
        out_shape=jax.ShapeDtypeStruct((groups * members, rows, wide), BF16),
        grid=(groups,),
        in_specs=[pl.BlockSpec(slices.shape, lambda i: (0, 0, 0))],
        out_specs=pl.BlockSpec((members, rows, wide), lambda i: (i, 0, 0)),
        scratch_shapes=[pltpu.VMEM((groups, wide // 2, members), F32)],
        compiler_params=pltpu.CompilerParams(vmem_limit_bytes=24 << 20),
        name="serve",
    )(slices)


def select_kernel(stride, place_ref, out_ref):
    place = place_ref[0:1] * stride + place_ref[1:2]
    column = jnp.transpose(jnp.broadcast_to(place.astype(F32), (8, place.shape[1])))[:, 0:1]
    out_ref[...] = jnp.where(column == iota(out_ref.shape, 1).astype(F32), 1.0, 0.0).astype(BF16)


def select(places, entries, groups, stride):
    return pl.pallas_call(
        lambda *refs: select_kernel(stride, *refs),
        out_shape=jax.ShapeDtypeStruct((entries, groups * stride), BF16),
        in_specs=[VMEM],
        out_specs=VMEM,
        name="select",
    )(places)


def arrange_kernel(couple, out_ref):
    for c in range(couple.shape[0]):
        mats = couple[c].astype(F32)
        tall = jnp.concatenate(
            [mats[:, j * 128 : (j + 1) * 128] for j in range(mats.shape[1] // 128)], axis=0
        )
        out_ref[c] = jnp.transpose(tall).astype(BF16)


def arrange(couple):
    count, fan, wide = couple.shape
    per_step = 8
    return pl.pallas_call(
        arrange_kernel,
        out_shape=jax.ShapeDtypeStruct((count, 128, wide * fan // 128), BF16),
        grid=(count // per_step,),
        in_specs=[pl.BlockSpec((per_step, fan, wide), lambda i: (i, 0, 0))],
        out_specs=pl.BlockSpec((per_step, 128, wide * fan // 128), lambda i: (i, 0, 0)),
        name="arrange",
    )(couple)


def pieces(value):
    high = value.astype(BF16).astype(F32)
    middle = (value - high).astype(BF16).astype(F32)
    return high, middle, value - high - middle


def near_kernel(offsets, before, own, following, out_ref, window, scale, rhs, lhs, kern):
    leaves, rows, size = out_ref.shape
    near = offsets.shape[0] // leaves
    one = jnp.ones((3, size), F32)
    zero = jnp.zeros((7, size), F32)
    for place, ref in enumerate((before, own, following)):

        def fill(i, carry, place=place, ref=ref):
            block = ref[:, pl.ds(pl.multiple_of(i * size, size), size)]
            window[place * leaves + i] = block[:rows]
            y = block[rows:].astype(F32)
            scale[place * leaves + i] = y[3:4]
            square = y[0:1] * y[0:1] + y[1:2] * y[1:2] + y[2:3] * y[2:3]
            rhs[place * leaves + i] = jnp.concatenate(
                [-2.0 * y[0:3], one, *pieces(square + SOFTEN), zero], axis=0
            ).astype(BF16)
            if place == 1:
                lhs[i] = jnp.transpose(
                    jnp.concatenate([y[0:3], *pieces(square), one, zero], axis=0)
                ).astype(BF16)
            return carry

        lax.fori_loop(0, leaves, fill, 0)

    def leaf(c, carry):
        for k in range(near):
            w = offsets[c * near + k]
            square = dot(lhs[c], rhs[w])
            kern[k] = (scale[w] * lax.rsqrt(square)).astype(BF16)
        total = jnp.zeros((rows, size), F32)
        for k in range(near):
            total += dot(window[offsets[c * near + k]], kern[k], NT)
        out_ref[c] = total
        return carry

    lax.fori_loop(0, leaves, leaf, 0)


def near_field(offsets, before, own, following, leaves, rows):
    size = own.shape[1] // leaves
    near = offsets.shape[0] // leaves
    return pl.pallas_call(
        near_kernel,
        out_shape=jax.ShapeDtypeStruct((leaves, rows, size), F32),
        in_specs=[SMEM, VMEM, VMEM, VMEM],
        out_specs=VMEM,
        scratch_shapes=[
            pltpu.VMEM((3 * leaves, rows, size), BF16),
            pltpu.VMEM((3 * leaves, 1, size), F32),
            pltpu.VMEM((3 * leaves, 16, size), BF16),
            pltpu.VMEM((leaves, size, 16), BF16),
            pltpu.VMEM((near, size, size), BF16),
        ],
        compiler_params=pltpu.CompilerParams(vmem_limit_bytes=40 << 20),
        cost_estimate=pl.CostEstimate(
            flops=20 * leaves * near * size * size * rows,
            bytes_accessed=6 << 20,
            transcendentals=leaves * near * size * size,
        ),
        name="near",
    )(offsets, before, own, following)


def final_kernel(counts, *refs):
    replies, refs = refs[: len(counts)], refs[len(counts) :]
    chosen, upper_mats, leaf_mats, down, basis, near, out_ref, taken, held, handed = refs
    uppers, leaves = upper_mats.shape[0], leaf_mats.shape[0]
    rank = down.shape[2]
    size = basis.shape[1] // leaves
    groups = handed.shape[0]
    members = replies[0].shape[0] // groups
    stride = taken.shape[1] // groups
    fan = chosen.shape[0] // (uppers + leaves)
    taken[...] = jnp.zeros(taken.shape, BF16)
    for m in range(members):
        first = 0
        for reply, count in zip(replies, counts):
            for g in range(groups):
                taken[m % 2, g * stride + first : g * stride + first + count] = reply[
                    g * members + m
                ]
            first += count
        block = dot(chosen[...], taken[m % 2]).reshape(uppers + leaves, fan, 2 * 2 * rank)
        held[:, m * 2 * fan : (m + 1) * 2 * fan] = jnp.concatenate(
            [block[:, :, : 2 * rank], block[:, :, 2 * rank :]], axis=1
        ).astype(BF16)
    for j in range(uppers):
        upper = folded(dot(upper_mats[j], held[leaves + j]), rank).astype(BF16)
        handed[j] = dot(down[j], upper)
    for c in range(leaves):
        cut = slice(c * size, (c + 1) * size)
        local = folded(dot(leaf_mats[c], held[c]), rank)
        local += handed[c // 4, c % 4 * rank : (c % 4 + 1) * rank]
        far = dot(local.astype(BF16), basis[:, cut], TN)
        out_ref[:, cut] = (far + near[c]).astype(BF16)


def final(replies, chosen, groups, upper_mats, leaf_mats, down, basis, near, shape):
    uppers, rank = down.shape[0], down.shape[2]
    counts = [reply.shape[1] for reply in replies]
    wide = upper_mats.shape[2]
    return pl.pallas_call(
        lambda *refs: final_kernel(counts, *refs),
        out_shape=jax.ShapeDtypeStruct(shape, BF16),
        in_specs=[VMEM] * (len(replies) + 6),
        out_specs=VMEM,
        scratch_shapes=[
            pltpu.VMEM((2, chosen.shape[1], replies[0].shape[2]), BF16),
            pltpu.VMEM((uppers + leaf_mats.shape[0], wide, 2 * rank), BF16),
            pltpu.VMEM((uppers, 4 * rank, rank), F32),
        ],
        compiler_params=pltpu.CompilerParams(vmem_limit_bytes=32 << 20),
        name="far",
    )(*replies, chosen, upper_mats, leaf_mats, down, basis, near)


def exchange(value, axes):
    return lax.all_to_all(value, axes, split_axis=0, concat_axis=0, tiled=True)


def body(
    density,
    points,
    weights,
    source_basis,
    target_basis,
    up_transfer,
    down_transfer,
    couple_leaf,
    couple_upper,
    owner_leaf,
    local_leaf,
    owner_upper,
    local_upper,
    near_list,
):
    devices = lax.axis_size(AXES)
    groups, members = lax.axis_size("gx"), lax.axis_size("gy")
    leaves, fan = owner_leaf.shape
    uppers = owner_upper.shape[0]
    vectors = density.shape[0]
    rank = source_basis.shape[0]
    half = rank // 2
    rows = leaves + uppers

    own = jnp.concatenate(
        [density, points, weights[None], jnp.zeros((4, density.shape[1]), BF16)], axis=0
    )
    before = passed_along(own, 1)
    following = passed_along(own, -1)

    asks, places = pl.pallas_call(
        request_kernel,
        out_shape=(
            jax.ShapeDtypeStruct((groups, 16, 256), BF16),
            jax.ShapeDtypeStruct((members, rows * fan), jnp.int32),
        ),
        in_specs=[VMEM] * 4,
        out_specs=(VMEM, VMEM),
        name="requests",
    )(owner_leaf.T, local_leaf.T, owner_upper.T, local_upper.T)
    asked = exchange(asks, "gx")

    slices = pl.pallas_call(
        multipole_kernel,
        out_shape=jax.ShapeDtypeStruct((members, rows, 4 * rank), BF16),
        in_specs=[VMEM] * 3,
        out_specs=VMEM,
        scratch_shapes=[
            pltpu.VMEM((rows * rank, vectors), F32),
            pltpu.VMEM((rows * half, 2 * vectors), F32),
            pltpu.VMEM((leaves * half, 2 * rank), F32),
        ],
        compiler_params=pltpu.CompilerParams(vmem_limit_bytes=16 << 20),
        name="multipoles",
    )(density, source_basis, up_transfer)
    asked = jnp.broadcast_to(asked[None, :, 0, :], (members, groups, asked.shape[2]))
    slices = exchange(jnp.concatenate([slices, asked], axis=1), "gy")

    leaf_mats = arrange(couple_leaf)
    upper_mats = arrange(couple_upper)
    slices, before, following, leaf_mats, upper_mats = lax.optimization_barrier(
        (slices, before, following, leaf_mats, upper_mats)
    )
    replies = exchange(serve(slices, groups, 0, SENT), AXES)

    offsets = (near_list - lax.axis_index(AXES) * leaves + leaves) % (leaves * devices)
    near = near_field(offsets.reshape(-1), before, own, following, leaves, vectors)
    down = (
        down_transfer.reshape(uppers, 4, rank, rank)
        .transpose(0, 1, 3, 2)
        .reshape(uppers, 4 * rank, rank)
    )
    chosen = select(places, rows * fan, groups, 64)

    def finish(received, picks):
        return final(
            received, picks, groups, upper_mats, leaf_mats, down, target_basis, near, density.shape
        )

    def some_left():
        others = exchange(serve(slices, groups, SENT, MOST - SENT), AXES)
        return finish((replies, others), select(places, rows * fan, groups, MOST))

    most = jnp.max(slices[:, rows:, 127].astype(F32))
    return lax.cond(most > SENT, some_left, lambda: finish((replies,), chosen))


def solution(mesh):
    whole = AXES
    placed = (
        P(None, whole),
        P(None, whole),
        P(whole),
        P(None, whole),
        P(None, whole),
        P(whole, None),
        P(whole, None),
        P(whole, None, None),
        P(whole, None, None),
        P(whole, None),
        P(whole, None),
        P(whole, None),
        P(whole, None),
        P(whole, None),
    )
    return jax.shard_map(
        body, mesh=mesh, in_specs=placed, out_specs=P(None, whole), check_vma=False
    )
```

time: 185 us -> 121 us (0.65)
  waiting for transfers between devices: 49.6 us -> 9.8 us
  local copies, waits for them, and re-layouts: 44.1 us -> 10.3 us
  Pallas kernels: 63.5 us -> 68 us
  other arithmetic: 2.14 us -> 4.48 us
  starting transfers between devices: 24.8 us -> 26.7 us
    ppermute x2, waiting for transfers between devices: 46.9 us -> 0.01 us  [passed_along(): return lax.ppermute(value, AXES, pairs)]
    reshape x10 -> x0, local copies, waits for them, and re-layouts: 33 us -> none  [the longest x4 16.5 us: coupled(): cut = mats.reshape(count, fan, 2, rank // 2, rank)]
    all_to_all x2 -> x3, waiting for transfers between devices: 2.7 us -> 9.8 us  [exchange(): return lax.all_to_all(value, axes, split_axis=0, concat_axis=0, tiled=True)]
    pallas_call x4 -> x7, Pallas kernels: 27.6 us -> 31 us  [the longest x1 15.4 us: final(): pl.pallas_call(lambda *refs: final_kernel(counts, *refs), out_shape=jax.S...]
    unnamed x24 -> x19, local copies, waits for them, and re-layouts: 6.88 us -> 4.42 us
    ppermute x2, starting transfers between devices: 5.82 us -> 7.76 us  [passed_along(): return lax.ppermute(value, AXES, pairs)]
    all_to_all x2 -> x3, starting transfers between devices: 19 us -> 18.9 us  [exchange(): return lax.all_to_all(value, axes, split_axis=0, concat_axis=0, tiled=True)]
  transfers between devices with their start and end apart: 4 -> 5, of which waited for: 2 -> 2; matrix products, arithmetic and copies ran while one was open for 20% -> 8% of each run, Pallas kernels for 22% -> 39%
where the time goes in v2:
time: 121 us; the launch traced here: 120 us
  Pallas kernels  68 us (56%)
  starting transfers between devices  26.7 us (22%)
  local copies, waits for them, and re-layouts  10.3 us (9%)
  waiting for transfers between devices  9.8 us (8%)
  other arithmetic  4.48 us (4%)
    pallas_call x1, Pallas kernels, near_field(): pl.pallas_call(near_kernel, out_shape=jax.ShapeDtypeStruct((leaves, rows,...  37 us
    all_to_all x3, starting transfers between devices, exchange(): return lax.all_to_all(value, axes, split_axis=0, concat_axis=0, tiled=True)  18.9 us
    pallas_call x1, Pallas kernels, final(): pl.pallas_call(lambda *refs: final_kernel(counts, *refs), out_shape=jax.S...  15.4 us
    all_to_all x3, waiting for transfers between devices, exchange(): return lax.all_to_all(value, axes, split_axis=0, concat_axis=0, tiled=True)  9.8 us
    ppermute x2, starting transfers between devices, passed_along(): return lax.ppermute(value, AXES, pairs)  7.76 us
    pallas_call x1, Pallas kernels, serve(): pl.pallas_call(lambda *refs: serve_kernel(first, *refs), out_shape=jax.Sh...  5.87 us
    pallas_call x2, Pallas kernels, arrange(): pl.pallas_call(arrange_kernel, out_shape=jax.ShapeDtypeStruct((count, 128...  4.83 us
    unnamed x19, local copies, waits for them, and re-layouts  4.42 us
  transfers between devices with their start and end apart: 5, of which 2 were waited for; matrix products, arithmetic and copies ran while one was open for 8% of the time, Pallas kernels for 39%

profile of v2, /device:TPU:1, one launch (start us, length us, event | category | flops | bytes accessed | tf_op | source)
XLA Modules:
  0.0 120.0 jit_solution(10632175645622786329)
XLA Ops:
  0.0 0.0 copy-start.1
  0.0 0.0 copy-start.8
  0.0 0.0 copy-start.9
  0.0 0.0 copy-start.4
  0.0 0.8 broadcast_in_dim.15
  0.9 0.1 pad.3.clone
  0.9 1.6 %maximum_maximum_fusion.own = bf16[72,8192]{1,0:T(8,128)(2,1)S(1)} fusion(bf16[1,8192]{1,0:T(2,128)(2,1)S(1)} %broadcast_in_dim.15, bf16[3,8192]{1,0:T(4,128)(2,1)} %param.17, bf16[64,8192]{1,0:T(8,128)(2,1)} %density.1, bf16[72]{0:T(256)(128)(2,1)S(1)} %pad.3.clone), kind=kLoop, calls=%fused_computation | loop fusion | flops 4718592 | bytes 2293904 | tf_op jit(solution)/shard_map/concatenate | solution.py:327
  2.5 2.2 %collective-permute-start = (bf16[72,8192]{1,0:T(8,128)(2,1)S(1)}, bf16[72,8192]{1,0:T(8,128)(2,1)}, u32[]{:S(2)}, u32[]{:S(2)}) collective-permute-start(bf16[72,8192]{1,0:T(8,128)(2,1)S(1)} %maximum_maximum_fusion.own), channel_id=1, source_target_pairs={{0,1},{1,2},{2,3},{3,4},{4,5},{5,6},{6,7},{7,8},{8,9},{9,10},{10,1... | collective-permute-start | bytes 3538952 | tf_op jit(solution)/shard_map/ppermute | solution.py:28
  4.7 5.6 %collective-permute-start.1 = (bf16[72,8192]{1,0:T(8,128)(2,1)S(1)}, bf16[72,8192]{1,0:T(8,128)(2,1)}, u32[]{:S(2)}, u32[]{:S(2)}) collective-permute-start(bf16[72,8192]{1,0:T(8,128)(2,1)S(1)} %maximum_maximum_fusion.own), channel_id=1, source_target_pairs={{0,127},{1,0},{2,1},{3,2},{4,3},{5,4},{6,5},{7,6},{8,7},{9,8},{10,... | collective-permute-start | bytes 3538952 | tf_op jit(solution)/shard_map/ppermute | solution.py:28
  10.3 0.0 copy-done.8
  10.3 0.7 copy.20
  10.9 0.0 copy-done.9
  10.9 0.7 copy.21
  11.6 1.8 %requests.1 = (bf16[8,16,256]{2,1,0:T(8,128)(2,1)}, s32[16,320]{1,0:T(8,128)}) custom-call(s32[8,32]{1,0:T(8,128)} %bitcast.15, s32[8,32]{1,0:T(8,128)} %bitcast.16, s32[8,8]{1,0:T(8,128)} %bitcast.13, s32[8,8]{1,0:T(8,128)} %bitcast.14), custom_call_target="tpu_custom_call" | custom-call | tf_op jit(solution)/shard_map/requests/pallas_call | solution.py:333
  13.4 5.3 %all-to-all-start.1 = ((bf16[8,16,256]{2,1,0:T(8,128)(2,1)}), bf16[8,16,256]{2,1,0:T(8,128)(2,1)S(1)}, u32[]{:S(2)}, u32[]{:S(2)}) async-start(bf16[8,16,256]{2,1,0:T(8,128)(2,1)} %get-tuple-element.60), calls=%async_computation.1 | async-start | bytes 131072 | tf_op jit(solution)/shard_map/all_to_all | solution.py:299
  18.7 0.0 copy-done.1
  18.7 0.0 copy-done.4
  18.7 0.0 copy-start.3
  18.7 1.2 %copy-done.3 = bf16[64,8192]{1,0:T(8,128)(2,1)S(1)} copy-done((bf16[64,8192]{1,0:T(8,128)(2,1)S(1)}, bf16[64,8192]{1,0:T(8,128)(2,1)}, u32[]{:S(2)}) %copy-start.3) | copy-done | bytes 1048600
  19.9 1.3 %multipoles.1 = bf16[16,40,256]{2,1,0:T(8,128)(2,1)S(1)} custom-call(bf16[64,8192]{1,0:T(8,128)(2,1)S(1)} %copy-done.1, bf16[64,8192]{1,0:T(8,128)(2,1)S(1)} %copy-done.3, bf16[32,4096]{1,0:T(8,128)(2,1)S(1)} %copy-done.4), custom_call_target="tpu_custom_call" | custom-call | tf_op jit(solution)/shard_map/multipoles/pallas_call | solution.py:345
  21.3 4.7 %all-to-all-done.1 = bf16[8,16,256]{2,1,0:T(8,128)(2,1)S(1)} async-done(((bf16[8,16,256]{2,1,0:T(8,128)(2,1)}), bf16[8,16,256]{2,1,0:T(8,128)(2,1)S(1)}, u32[]{:S(2)}, u32[]{:S(2)}) %all-to-all-start.1) | async-done | bytes 65568 | tf_op jit(solution)/shard_map/all_to_all | solution.py:299
  26.0 0.8 pad_maximum_fusion
  26.7 4.2 %all-to-all-start.2 = ((bf16[16,48,256]{2,1,0:T(8,128)(2,1)}), bf16[16,48,256]{2,1,0:T(8,128)(2,1)}, u32[]{:S(2)}, u32[]{:S(2)}) async-start(bf16[16,48,256]{2,1,0:T(8,128)(2,1)} %pad_maximum_fusion), calls=%async_computation.2 | async-start | bytes 786432 | tf_op jit(solution)/shard_map/all_to_all | solution.py:299
  31.0 2.8 %arrange.2 = bf16[32,128,256]{2,1,0:T(8,128)(2,1)S(1)} custom-call(bf16[32,8,4096]{2,1,0:T(8,128)(2,1)} %couple.2), custom_call_target="tpu_custom_call" | custom-call | tf_op jit(solution)/shard_map/arrange/pallas_call | solution.py:166
  33.7 2.0 %arrange.3 = bf16[8,128,256]{2,1,0:T(8,128)(2,1)} custom-call(bf16[8,8,4096]{2,1,0:T(8,128)(2,1)} %couple.3), custom_call_target="tpu_custom_call" | custom-call | tf_op jit(solution)/shard_map/arrange/pallas_call | solution.py:166
  35.8 5.1 %all-to-all-done.2.refs_0_ = bf16[16,48,256]{2,1,0:T(8,128)(2,1)} async-done(((bf16[16,48,256]{2,1,0:T(8,128)(2,1)}), bf16[16,48,256]{2,1,0:T(8,128)(2,1)}, u32[]{:S(2)}, u32[]{:S(2)}) %all-to-all-start.2) | async-done | bytes 393248 | tf_op jit(solution)/shard_map/all_to_all | solution.py:299
  40.9 0.0 collective-permute-done.before
  40.9 0.0 collective-permute-done.1.following
  40.9 5.9 %serve.3 = bf16[128,56,256]{2,1,0:T(8,128)(2,1)S(1)} custom-call(bf16[16,48,256]{2,1,0:T(8,128)(2,1)} %all-to-all-done.2.refs_0_), custom_call_target="tpu_custom_call" | custom-call | tf_op jit(solution)/shard_map/serve/pallas_call | solution.py:126
  46.8 0.0 copy-start
  46.8 1.8 %copy-done = bf16[128,56,256]{2,1,0:T(8,128)(2,1)} copy-done((bf16[128,56,256]{2,1,0:T(8,128)(2,1)}, bf16[128,56,256]{2,1,0:T(8,128)(2,1)S(1)}, u32[]{:S(2)}) %copy-start) | copy-done | bytes 3670040
  48.7 0.0 copy-start.6
  48.7 9.5 %all-to-all-start.3 = ((bf16[128,56,256]{2,1,0:T(8,128)(2,1)}), bf16[128,56,256]{2,1,0:T(8,128)(2,1)}, u32[]{:S(2)}, u32[]{:S(2)}) async-start(bf16[128,56,256]{2,1,0:T(8,128)(2,1)} %copy-done), calls=%async_computation.3 | async-start | bytes 7340032 | tf_op jit(solution)/shard_map/all_to_all | solution.py:299
  58.1 0.7 add_select_fusion
  58.9 0.7 copy.23
  59.6 0.8 reshape.12.offsets
  60.4 0.0 copy-done.6
  60.4 1.3 %reshape.10 = bf16[8,4,64,64]{3,2,1,0:T(8,128)(2,1)} reshape(bf16[32,4096]{1,0:T(8,128)(2,1)S(1)} %copy-done.6) | data formatting | bytes 524288 | tf_op jit(solution)/shard_map/reshape | solution.py:371
  61.7 2.1 %copy.22 = bf16[8,4,64,64]{2,3,1,0:T(8,128)(2,1)} copy(bf16[8,4,64,64]{3,2,1,0:T(8,128)(2,1)} %reshape.10) | data formatting | bytes 524288 | tf_op jit(solution)/shard_map/reshape | solution.py:371
  63.8 1.7 %select.5 = bf16[320,512]{1,0:T(8,128)(2,1)} custom-call(s32[16,320]{1,0:T(8,128)} %get-tuple-element.62.refs_0_), custom_call_target="tpu_custom_call" | custom-call | tf_op jit(solution)/shard_map/select/pallas_call | solution.py:145
  65.5 1.5 %slice_reduce_fusion = bf16[]{:T(256)} fusion(bf16[16,48,256]{2,1,0:T(8,128)(2,1)} %all-to-all-done.2.refs_0_), kind=kLoop, calls=%fused_computation.2 | loop fusion | flops 127 | bytes 258 | tf_op jit(solution)/shard_map/reduce_max | solution.py:386
  67.6 0.0 copy-start.7
  67.6 37.0 %near.1 = f32[32,64,256]{2,1,0:T(8,128)} custom-call(s32[288]{0:T(512)S(1)} %reshape.12.offsets, bf16[72,8192]{1,0:T(8,128)(2,1)} %collective-permute-done.before, bf16[72,8192]{1,0:T(8,128)(2,1)S(1)} %maximum_maximum_fusion.own, bf16[72,8192]{1,0:T(8,128)(2,1)} %collective-permute-done.1.following), custom_call_target="tpu_custom_call" | custom-call | flops 24159191040 | bytes 6291456 | tf_op jit(solution)/shard_map/near/pallas_call | solution.py:223
  104.6 0.0 all-to-all-done.3
  104.6 0.0 copy-done.7
  104.6 15.4 %conditional.1 = (bf16[64,8192]{1,0:T(8,128)(2,1)}) conditional(s32[]{:T(128)} %convert_element_type.4, (bf16[128,56,256]{2,1,0:T(8,128)(2,1)}, bf16[320,512]{1,0:T(8,128)(2,1)}, bf16[8,128,256]{2,1,0:T(8,128)(2,1)}, bf16[32,128,256]{2,1,0:T(8,128)(2,1)S(1)}, bf16[8,256,64]{2,1,0:T(8,128)(2,1)}, /*index=5*/bf16[64,8192]{1,0:T(8,128)(2,1)}, ...), branch_computations={%region_1.2_spmd, %region_2.3_spmd} | conditional | bytes 14745696 | solution.py:387
  104.6 15.4 %far.2 = bf16[64,8192]{1,0:T(8,128)(2,1)} custom-call(bf16[128,56,256]{2,1,0:T(8,128)(2,1)} %get-tuple-element.38.refs_0_, bf16[320,512]{1,0:T(8,128)(2,1)} %get-tuple-element.39.refs_1_, bf16[8,128,256]{2,1,0:T(8,128)(2,1)} %get-tuple-element.40.refs_2_, bf16[32,128,256]{2,1,0:T(8,128)(2,1)S(1)} %get-tuple-element.41.refs_3_, ...), custom_call_target="tpu_custom_call" | custom-call | tf_op jit(solution)/shard_map/cond/branch_0_fun/far/pallas_call | solution.py:283
  (4 shorter events, 0.0 us)
Async XLA Ops:
  0.0 18.7 %copy-start.1 = (bf16[64,8192]{1,0:T(8,128)(2,1)S(1)}, bf16[64,8192]{1,0:T(8,128)(2,1)}, u32[]{:S(2)}) copy-start(bf16[64,8192]{1,0:T(8,128)(2,1)} %density.1) | copy-start | bytes 3145732
  0.0 10.3 %copy-start.8 = (s32[8,8]{1,0:T(8,128)S(1)}, s32[8,8]{1,0:T(8,128)}, u32[]{:S(2)}) copy-start(s32[8,8]{1,0:T(8,128)} %param.27) | copy-start | bytes 772
  0.0 10.9 %copy-start.9 = (s32[8,8]{1,0:T(8,128)S(1)}, s32[8,8]{1,0:T(8,128)}, u32[]{:S(2)}) copy-start(s32[8,8]{1,0:T(8,128)} %param.28) | copy-start | bytes 772
  0.0 18.7 %copy-start.4 = (bf16[32,4096]{1,0:T(8,128)(2,1)S(1)}, bf16[32,4096]{1,0:T(8,128)(2,1)}, u32[]{:S(2)}) copy-start(bf16[32,4096]{1,0:T(8,128)(2,1)} %up_ref.1) | copy-start | bytes 786436
  2.5 38.4 %collective-permute-start = (bf16[72,8192]{1,0:T(8,128)(2,1)S(1)}, bf16[72,8192]{1,0:T(8,128)(2,1)}, u32[]{:S(2)}, u32[]{:S(2)}) collective-permute-start(bf16[72,8192]{1,0:T(8,128)(2,1)S(1)} %maximum_maximum_fusion.own), channel_id=1, source_target_pairs={{0,1},{1,2},{2,3},{3,4},{4,5},{5,6},{6,7},{7,8},{8,9},{9,10},{10,1... | collective-permute-start | bytes 3538952 | tf_op jit(solution)/shard_map/ppermute | solution.py:28
  4.7 36.2 %collective-permute-start.1 = (bf16[72,8192]{1,0:T(8,128)(2,1)S(1)}, bf16[72,8192]{1,0:T(8,128)(2,1)}, u32[]{:S(2)}, u32[]{:S(2)}) collective-permute-start(bf16[72,8192]{1,0:T(8,128)(2,1)S(1)} %maximum_maximum_fusion.own), channel_id=1, source_target_pairs={{0,127},{1,0},{2,1},{3,2},{4,3},{5,4},{6,5},{7,6},{8,7},{9,8},{10,... | collective-permute-start | bytes 3538952 | tf_op jit(solution)/shard_map/ppermute | solution.py:28
  13.4 12.5 %all-to-all-start.1 = ((bf16[8,16,256]{2,1,0:T(8,128)(2,1)}), bf16[8,16,256]{2,1,0:T(8,128)(2,1)S(1)}, u32[]{:S(2)}, u32[]{:S(2)}) async-start(bf16[8,16,256]{2,1,0:T(8,128)(2,1)} %get-tuple-element.60), calls=%async_computation.1 | async-start | bytes 131072 | tf_op jit(solution)/shard_map/all_to_all | solution.py:299
  18.7 1.2 %copy-start.3 = (bf16[64,8192]{1,0:T(8,128)(2,1)S(1)}, bf16[64,8192]{1,0:T(8,128)(2,1)}, u32[]{:S(2)}) copy-start(bf16[64,8192]{1,0:T(8,128)(2,1)} %basis.1) | copy-start | bytes 3145732
  26.7 14.2 %all-to-all-start.2 = ((bf16[16,48,256]{2,1,0:T(8,128)(2,1)}), bf16[16,48,256]{2,1,0:T(8,128)(2,1)}, u32[]{:S(2)}, u32[]{:S(2)}) async-start(bf16[16,48,256]{2,1,0:T(8,128)(2,1)} %pad_maximum_fusion), calls=%async_computation.2 | async-start | bytes 786432 | tf_op jit(solution)/shard_map/all_to_all | solution.py:299
  46.8 1.9 %copy-start = (bf16[128,56,256]{2,1,0:T(8,128)(2,1)}, bf16[128,56,256]{2,1,0:T(8,128)(2,1)S(1)}, u32[]{:S(2)}) copy-start(bf16[128,56,256]{2,1,0:T(8,128)(2,1)S(1)} %serve.3) | copy-start | bytes 11010052
  48.7 11.7 %copy-start.6 = (bf16[32,4096]{1,0:T(8,128)(2,1)S(1)}, bf16[32,4096]{1,0:T(8,128)(2,1)}, u32[]{:S(2)}) copy-start(bf16[32,4096]{1,0:T(8,128)(2,1)} %param.22) | copy-start | bytes 786436
  48.7 55.9 %all-to-all-start.3 = ((bf16[128,56,256]{2,1,0:T(8,128)(2,1)}), bf16[128,56,256]{2,1,0:T(8,128)(2,1)}, u32[]{:S(2)}, u32[]{:S(2)}) async-start(bf16[128,56,256]{2,1,0:T(8,128)(2,1)} %copy-done), calls=%async_computation.3 | async-start | bytes 7340032 | tf_op jit(solution)/shard_map/all_to_all | solution.py:299
  67.6 37.0 %copy-start.7 = (s32[16,320]{1,0:T(8,128)S(1)}, s32[16,320]{1,0:T(8,128)}, u32[]{:S(2)}) copy-start(s32[16,320]{1,0:T(8,128)} %get-tuple-element.62.refs_0_) | copy-start | bytes 61444

commit v3 on v2

v3 whole, which is shorter than its diff:
```python
import jax
import jax.numpy as jnp
from jax import lax
from jax.experimental import pallas as pl
from jax.experimental.pallas import tpu as pltpu
from jax.sharding import PartitionSpec as P

SOFTEN = 0.0025
AXES = ("gx", "gy")
SENT = 28
MOST = 40
F32 = jnp.float32
BF16 = jnp.bfloat16
NN = (((1,), (0,)), ((), ()))
NT = (((1,), (1,)), ((), ()))
TN = (((0,), (0,)), ((), ()))
VMEM = pl.BlockSpec(memory_space=pltpu.VMEM)
ANY = pl.BlockSpec(memory_space=pl.ANY)
ROOM = 60 << 20
SMEM = pl.BlockSpec(memory_space=pltpu.SMEM)


def dot(a, b, dims=NN):
    return lax.dot_general(a, b, dims, preferred_element_type=F32)


def passed_along(value, steps):
    count = lax.axis_size(AXES)
    pairs = [(source, (source + steps) % count) for source in range(count)]
    return lax.ppermute(value, AXES, pairs)


def iota(shape, dim):
    return lax.broadcasted_iota(jnp.int32, shape, dim)


def folded(pair, rank):
    return pair[:rank, :rank] + pair[rank:, rank:]


def flat_row(table):
    wide, rows = table.shape
    spread = (iota((rows, rows * wide), 1) // wide == iota((rows, rows * wide), 0)).astype(BF16)
    keep = iota((wide, rows * wide), 1) % wide == iota((wide, rows * wide), 0)
    return jnp.sum(
        jnp.where(keep, dot(table.astype(F32).astype(BF16), spread), 0.0), axis=0, keepdims=True
    ).astype(jnp.int32)


def request_kernel(own_leaf, loc_leaf, own_upper, loc_upper, ask_ref, place_ref):
    groups = ask_ref.shape[0]
    leaves, uppers = own_leaf.shape[1], own_upper.shape[0]
    tall_owner, tall_row = jnp.transpose(own_upper[...]), jnp.transpose(loc_upper[...])
    owner = jnp.concatenate([flat_row(own_leaf[...]), flat_row(tall_owner)], axis=1)
    row = jnp.concatenate([flat_row(loc_leaf[...]), flat_row(tall_row) + leaves], axis=1)
    entries = owner.shape[1]
    member = owner // groups
    group = owner - member * groups
    hit = group == iota((groups, entries), 0)
    ones = hit.astype(BF16)
    before = (iota((entries, entries), 0) < iota((entries, entries), 1)).astype(BF16)
    rank = jnp.sum(jnp.where(hit, dot(ones, before), 0.0), axis=0, keepdims=True).astype(jnp.int32)
    slot = jnp.where(rank < SENT, rank, rank + SENT)
    second = slot + jnp.where(rank < SENT, SENT, MOST - SENT)
    first_here = slot == iota((128, entries), 0)
    second_here = second == iota((128, entries), 0)
    far_row = row + (leaves + uppers)
    members = jnp.where(first_here | second_here, member, 0)
    rows = jnp.where(first_here, row, jnp.where(second_here, far_row, 0))
    wanted = [dot(ones, part.astype(F32).astype(BF16), NT) for part in (members, rows)]
    most = jnp.max(jnp.sum(hit.astype(F32), axis=1, keepdims=True), axis=0, keepdims=True)
    wanted[0] = jnp.where(iota((groups, 128), 1) == 127, most, wanted[0])
    both = jnp.concatenate(wanted, axis=1)
    for g in range(groups):
        ask_ref[g] = jnp.broadcast_to(both[g : g + 1], ask_ref.shape[1:]).astype(BF16)
    place_ref[...] = jnp.where(iota(place_ref.shape, 0) == 0, group, rank)


def multipole_kernel(density, basis, up_ref, out_ref, square, table, up):
    leaves = up_ref.shape[0]
    rank = square.shape[1]
    half = rank // 2
    rows = table.shape[0] // half
    size = density.shape[1] // leaves
    for leaf in range(leaves):
        cut = slice(leaf * size, (leaf + 1) * size)
        square[leaf * rank : (leaf + 1) * rank] = dot(basis[:, cut], density[:, cut], NT)

    def pack(first, count):
        even = square[pl.ds(first * rank, count * half, stride=2)]
        odd = square[pl.ds(first * rank + 1, count * half, stride=2)]
        table[first * half : (first + count) * half] = jnp.concatenate([even, odd], axis=1)

    pack(0, leaves)
    for j in range(half):
        up[pl.ds(j, leaves, stride=half)] = up_ref[:, j * 2 * rank : (j + 1) * 2 * rank].astype(F32)
    for upper in range(rows - leaves):
        cut = slice(upper * 4 * half, (upper + 1) * 4 * half)
        pair = dot(up[cut].astype(BF16), table[cut].astype(BF16), TN)
        square[(leaves + upper) * rank : (leaves + upper + 1) * rank] = folded(pair, rank)
    pack(leaves, rows - leaves)
    for m in range(out_ref.shape[0]):
        parts = [table[pl.ds(4 * m + a, rows, stride=half)] for a in range(4)]
        pairs = [jnp.concatenate(parts[:2], axis=1), jnp.concatenate(parts[2:], axis=1)]
        out_ref[m] = jnp.concatenate(pairs, axis=0).astype(BF16)


def serve_kernel(first, slices, out_ref, codes):
    step = pl.program_id(0)
    members, count, wide = slices.shape
    rows = out_ref.shape[1]
    asking = codes.shape[2]
    some = out_ref.shape[0] // asking

    @pl.when(step == 0)
    def _():
        asked = slices[:, count - asking :, :].astype(F32)
        code = asked[:, :, : wide // 2] * count + asked[:, :, wide // 2 :]
        for m in range(members):
            codes[m] = jnp.transpose(code[m])

    lanes = iota((rows, members * count), 1).astype(F32)
    table = slices[...].reshape(members * count, wide)
    for m in range(some):
        column = codes[step * some + m, first : first + rows]
        for t in range(0, asking, 4):
            picks = jnp.concatenate(
                [jnp.where(column[:, u : u + 1] == lanes, 1.0, 0.0) for u in range(t, t + 4)],
                axis=0,
            ).astype(BF16)
            out_ref[m * asking + t : m * asking + t + 4] = (
                dot(picks, table).reshape(4, rows, wide).astype(BF16)
            )


def serve(slices, asking, first, rows):
    members, count, wide = slices.shape
    some = members // 2
    return pl.pallas_call(
        lambda *refs: serve_kernel(first, *refs),
        out_shape=jax.ShapeDtypeStruct((members * asking, rows, wide), BF16),
        grid=(members // some,),
        in_specs=[pl.BlockSpec(slices.shape, lambda i: (0, 0, 0))],
        out_specs=pl.BlockSpec((some * asking, rows, wide), lambda i: (i, 0, 0)),
        scratch_shapes=[pltpu.VMEM((members, wide // 2, asking), F32)],
        compiler_params=pltpu.CompilerParams(vmem_limit_bytes=ROOM),
        name="serve",
    )(slices)


def arrange_kernel(couple, out_ref):
    for c in range(couple.shape[0]):
        mats = couple[c].astype(F32)
        tall = jnp.concatenate(
            [mats[:, j * 128 : (j + 1) * 128] for j in range(mats.shape[1] // 128)], axis=0
        )
        out_ref[c] = jnp.transpose(tall).astype(BF16)


def arrange(couple):
    count, fan, wide = couple.shape
    per_step = 8
    return pl.pallas_call(
        arrange_kernel,
        out_shape=jax.ShapeDtypeStruct((count, 128, wide * fan // 128), BF16),
        grid=(count // per_step,),
        in_specs=[pl.BlockSpec((per_step, fan, wide), lambda i: (i, 0, 0))],
        out_specs=pl.BlockSpec((per_step, 128, wide * fan // 128), lambda i: (i, 0, 0)),
        compiler_params=pltpu.CompilerParams(vmem_limit_bytes=ROOM),
        name="arrange",
    )(couple)


def pieces(value):
    high = value.astype(BF16).astype(F32)
    middle = (value - high).astype(BF16).astype(F32)
    return high, middle, value - high - middle


def near_kernel(listed, first, before, own, following, out_ref, window, sources, targets, kern):
    leaves, rows, size = out_ref.shape
    near = listed.shape[0]
    wide = own.shape[1]
    total = first[1]
    one = jnp.ones((3, wide), F32)
    zero = jnp.zeros((6, wide), F32)
    for place, ref in enumerate((before, own, following)):
        cut = slice(place * wide, (place + 1) * wide)
        window[:, cut] = ref[:rows]
        y = ref[rows:].astype(F32)
        square = y[0:1] * y[0:1] + y[1:2] * y[1:2] + y[2:3] * y[2:3]
        sources[cut] = jnp.transpose(
            jnp.concatenate([-2.0 * y[0:3], one, *pieces(square + SOFTEN), y[3:4], zero], axis=0)
        ).astype(BF16)
        if place == 1:
            targets[...] = jnp.concatenate(
                [y[0:3], *pieces(square), one, zero, zero[:1]], axis=0
            ).astype(BF16)

    def span(leaf):
        return pl.ds(pl.multiple_of(leaf * size, size), size)

    def place_of(c, k):
        offset = listed[k, c] - first[0] + leaves
        offset = jnp.where(offset < 0, offset + total, offset)
        return span(jnp.where(offset >= total, offset - total, offset))

    def fill(c, k, slot):
        block = sources[place_of(c, k)]
        square = dot(block, targets[:, span(c)])
        kern[slot, k] = (block[:, 9:10].astype(F32) * lax.rsqrt(square)).astype(BF16)

    def both(filled, used, slot):
        sum_ = jnp.zeros((rows, size), F32)
        for k in range(near):
            fill(filled, k, 1 - slot)
            sum_ += dot(window[:, place_of(used, k)], kern[slot, k])
        out_ref[used] = sum_

    for k in range(near):
        fill(0, k, 0)

    def two(i, carry):
        both(2 * i + 1, 2 * i, 0)
        both(jnp.minimum(2 * i + 2, leaves - 1), 2 * i + 1, 1)
        return carry

    lax.fori_loop(0, leaves // 2, two, 0)


def near_field(listed, first, before, own, following, leaves, rows):
    wide = own.shape[1]
    size = wide // leaves
    near = listed.shape[0]
    return pl.pallas_call(
        near_kernel,
        out_shape=jax.ShapeDtypeStruct((leaves, rows, size), F32),
        in_specs=[SMEM, SMEM, VMEM, VMEM, VMEM],
        out_specs=VMEM,
        scratch_shapes=[
            pltpu.VMEM((rows, 3 * wide), BF16),
            pltpu.VMEM((3 * wide, 16), BF16),
            pltpu.VMEM((16, wide), BF16),
            pltpu.VMEM((2, near, size, size), BF16),
        ],
        compiler_params=pltpu.CompilerParams(vmem_limit_bytes=ROOM),
        cost_estimate=pl.CostEstimate(
            flops=400 * leaves * near * size * size * rows,
            bytes_accessed=6 << 20,
            transcendentals=leaves * near * size * size,
        ),
        name="near",
    )(listed, first, before, own, following)


def final_kernel(groups, places, *refs):
    count = (len(refs) - 5) // 2
    sources, out_ref, refs = refs[: count - 1], refs[count - 1], refs[count:]
    targets, out_here, (taken, held, handed, sems, out_sems) = (
        refs[: count - 1],
        refs[count - 1],
        refs[count:],
    )
    replies = targets[:-5]
    upper_mats, down, leaf_mats, basis, near = targets[-5:]
    uppers, leaves = upper_mats.shape[0], leaf_mats.shape[0]
    entries, rank = places.shape[1], down.shape[2]
    members = replies[0].shape[0] // groups
    size = basis.shape[1] // leaves
    fan = entries // (uppers + leaves)
    parts = out_sems.shape[0]
    loads = [
        pltpu.make_async_copy(source, target, sems.at[i])
        for i, (source, target) in enumerate(zip(sources, targets))
    ]
    for load in loads:
        load.start()
    group = jnp.transpose(places[...].astype(F32))
    group, position = group[:, 0:1], group[:, 1:2]
    first = 0
    for number, reply in enumerate(replies):
        rows = reply.shape[1] // 2
        stride = (rows + 15) // 16 * 16
        lane = iota((entries, groups * stride), 1).astype(F32)
        inside = (position >= first) & (position < first + rows)
        wanted = jnp.where(inside, group * stride + position - first, -1.0)
        chosen = jnp.where(wanted == lane, 1.0, 0.0).astype(BF16)
        first += rows
        taken[...] = jnp.zeros(taken.shape, BF16)
        loads[number].wait()
        for m in range(2 * members):
            for g in range(groups):
                taken[m % 2, g * stride : g * stride + rows] = reply[
                    m // 2 * groups + g, m % 2 * rows : (m % 2 + 1) * rows
                ]
            block = dot(chosen, taken[m % 2, : groups * stride])
            block = block.reshape(uppers + leaves, fan, 4 * rank)
            block = jnp.concatenate([block[:, :, : 2 * rank], block[:, :, 2 * rank :]], axis=1)
            cut = slice(m * 2 * fan, (m + 1) * 2 * fan)
            if number == 0:
                held[:, cut] = block.astype(BF16)
            else:
                held[:, cut] += block.astype(BF16)
    loads = loads[len(replies) :]
    loads[0].wait()
    loads[1].wait()
    for j in range(uppers):
        upper = folded(dot(upper_mats[j], held[leaves + j]), rank).astype(BF16)
        handed[j] = dot(down[j], upper)
    loads[2].wait()
    locals_ = []
    for c in range(leaves):
        local = folded(dot(leaf_mats[c], held[c]), rank)
        locals_.append(local + handed[c // 4, c % 4 * rank : (c % 4 + 1) * rank])
    tall = jnp.transpose(jnp.concatenate(locals_, axis=0)).astype(BF16)
    loads[3].wait()
    loads[4].wait()
    stores = []
    for part in range(parts):
        begin = part * leaves // parts
        for c in range(begin, begin + leaves // parts):
            cut = slice(c * size, (c + 1) * size)
            far = dot(tall[:, c * rank : (c + 1) * rank], basis[:, cut])
            out_here[:, cut] = (far + near[c]).astype(BF16)
        cut = pl.ds(begin * size, leaves * size // parts)
        stores.append(
            pltpu.make_async_copy(out_here.at[:, cut], out_ref.at[:, cut], out_sems.at[part])
        )
        stores[-1].start()
    for store in stores:
        store.wait()


def final(groups, places, replies, upper_mats, down, leaf_mats, basis, near):
    uppers, rank = down.shape[0], down.shape[2]
    operands = (*replies, upper_mats, down, leaf_mats, basis, near)
    out = jax.ShapeDtypeStruct((near.shape[1], basis.shape[1]), BF16)
    parts = 4
    return pl.pallas_call(
        lambda *refs: final_kernel(groups, *refs),
        out_shape=out,
        in_specs=[VMEM] + [ANY] * len(operands),
        out_specs=ANY,
        scratch_shapes=[pltpu.VMEM(x.shape, x.dtype) for x in (*operands, out)]
        + [
            pltpu.VMEM((2, groups * 32, replies[0].shape[2]), BF16),
            pltpu.VMEM((uppers + leaf_mats.shape[0], upper_mats.shape[2], 2 * rank), BF16),
            pltpu.VMEM((uppers, 4 * rank, rank), F32),
            pltpu.SemaphoreType.DMA((len(operands),)),
            pltpu.SemaphoreType.DMA((parts,)),
        ],
        compiler_params=pltpu.CompilerParams(vmem_limit_bytes=ROOM),
        name="far",
    )(places, *operands)


def exchange(value, axes):
    return lax.all_to_all(value, axes, split_axis=0, concat_axis=0, tiled=True)


def body(
    density,
    points,
    weights,
    source_basis,
    target_basis,
    up_transfer,
    down_transfer,
    couple_leaf,
    couple_upper,
    owner_leaf,
    local_leaf,
    owner_upper,
    local_upper,
    near_list,
):
    devices = lax.axis_size(AXES)
    members, groups = lax.axis_size("gx"), lax.axis_size("gy")
    leaves, fan = owner_leaf.shape
    uppers = owner_upper.shape[0]
    vectors = density.shape[0]
    rank = source_basis.shape[0]
    half = rank // 2
    rows = leaves + uppers

    asks, places = pl.pallas_call(
        request_kernel,
        out_shape=(
            jax.ShapeDtypeStruct((groups, 16, 256), BF16),
            jax.ShapeDtypeStruct((8, rows * fan), jnp.int32),
        ),
        in_specs=[VMEM] * 4,
        out_specs=(VMEM, VMEM),
        name="requests",
    )(owner_leaf.T, local_leaf.T, owner_upper, local_upper)
    asked = exchange(asks, "gy")
    slices = pl.pallas_call(
        multipole_kernel,
        out_shape=jax.ShapeDtypeStruct((members, 2 * rows, 4 * rank), BF16),
        in_specs=[VMEM] * 3,
        out_specs=VMEM,
        scratch_shapes=[
            pltpu.VMEM((rows * rank, vectors), F32),
            pltpu.VMEM((rows * half, 2 * vectors), F32),
            pltpu.VMEM((leaves * half, 2 * rank), F32),
        ],
        compiler_params=pltpu.CompilerParams(vmem_limit_bytes=ROOM),
        name="multipoles",
    )(density, source_basis, up_transfer)

    slices, asked, density, points, weights = lax.optimization_barrier(
        (slices, asked, density, points, weights)
    )
    own = jnp.concatenate(
        [density, points, weights[None], jnp.zeros((4, density.shape[1]), BF16)], axis=0
    )
    before = passed_along(own, 1)
    following = passed_along(own, -1)
    asked = jnp.broadcast_to(asked[None, :, 0, :], (members, groups, asked.shape[2]))
    slices = jnp.concatenate([slices, asked], axis=1)

    slices, own, couple_leaf, couple_upper, down_transfer = lax.optimization_barrier(
        (slices, own, couple_leaf, couple_upper, down_transfer)
    )
    slices = exchange(slices, "gx")
    upper_mats = arrange(couple_upper)
    leaf_mats = arrange(couple_leaf)
    down = (
        down_transfer.reshape(uppers, 4, rank, rank)
        .transpose(0, 1, 3, 2)
        .reshape(uppers, 4 * rank, rank)
    )
    first = jnp.stack([lax.axis_index(AXES) * leaves, jnp.int32(leaves * devices)])
    slices, leaf_mats, upper_mats, down, first = lax.optimization_barrier(
        (slices, leaf_mats, upper_mats, down, first)
    )
    replies = exchange(serve(slices, groups, 0, 2 * SENT), AXES)
    near = near_field(near_list.T, first, before, own, following, leaves, vectors)
    most = jnp.max(slices[:, 2 * rows :, 127].astype(F32))

    def finish(*received):
        return final(groups, places, received, upper_mats, down, leaf_mats, target_basis, near)

    def some_left():
        others = exchange(serve(slices, groups, 2 * SENT, 2 * (MOST - SENT)), AXES)
        return finish(replies, others)

    return lax.cond(most > SENT, some_left, lambda: finish(replies))


def solution(mesh):
    whole = AXES
    placed = (
        P(None, whole),
        P(None, whole),
        P(whole),
        P(None, whole),
        P(None, whole),
        P(whole, None),
        P(whole, None),
        P(whole, None, None),
        P(whole, None, None),
        P(whole, None),
        P(whole, None),
        P(whole, None),
        P(whole, None),
        P(whole, None),
    )
    return jax.shard_map(
        body, mesh=mesh, in_specs=placed, out_specs=P(None, whole), check_vma=False
    )
```

time: 121 us -> 109 us (0.901)
  Pallas kernels: 68 us -> 46.8 us
  waiting for transfers between devices: 9.8 us -> 29.3 us
  local copies, waits for them, and re-layouts: 10.3 us -> 1.74 us
  other arithmetic: 4.48 us -> 2.41 us
    all_to_all x3, waiting for transfers between devices: 9.8 us -> 29.3 us  [exchange(): return lax.all_to_all(value, axes, split_axis=0, concat_axis=0, tiled=True)]
    pallas_call x1, Pallas kernels: 37 us -> 23.8 us  [near_field(): pl.pallas_call(near_kernel, out_shape=jax.ShapeDtypeStruct((leaves, rows,...]
    pallas_call x2 -> x1, Pallas kernels: 17.1 us -> 6.42 us  [final(): pl.pallas_call(lambda *refs: final_kernel(groups, *refs), out_shape=out,...]
    unnamed x19 -> x25, local copies, waits for them, and re-layouts: 4.42 us -> 0.05 us
    all_to_all x3, starting transfers between devices: 18.9 us -> 22.2 us  [exchange(): return lax.all_to_all(value, axes, split_axis=0, concat_axis=0, tiled=True)]
    ppermute x2, starting transfers between devices: 7.76 us -> 5.14 us  [passed_along(): return lax.ppermute(value, AXES, pairs)]
    pallas_call x1, Pallas kernels: 1.35 us -> 3.63 us  [body(): pl.pallas_call(multipole_kernel, out_shape=jax.ShapeDtypeStruct((members,...]
    reshape x2, local copies, waits for them, and re-layouts: 3.4 us -> 1.57 us  [body(): down_transfer.reshape(uppers, 4, rank, rank).transpose(0, 1, 3, 2)]
  transfers between devices with their start and end apart: 5 -> 5, of which waited for: 2 -> 3; matrix products, arithmetic and copies ran while one was open for 8% -> 3% of each run, Pallas kernels for 39% -> 35%
where the time goes in v3:
time: 109 us
  Pallas kernels  46.8 us (43%)
  waiting for transfers between devices  29.3 us (27%)
  starting transfers between devices  27.4 us (25%)
  other arithmetic  2.41 us (2%)
  local copies, waits for them, and re-layouts  1.74 us (2%)
    all_to_all x3, waiting for transfers between devices, exchange(): return lax.all_to_all(value, axes, split_axis=0, concat_axis=0, tiled=True)  29.3 us
    pallas_call x1, Pallas kernels, near_field(): pl.pallas_call(near_kernel, out_shape=jax.ShapeDtypeStruct((leaves, rows,...  23.8 us
    all_to_all x3, starting transfers between devices, exchange(): return lax.all_to_all(value, axes, split_axis=0, concat_axis=0, tiled=True)  22.2 us
    pallas_call x1, Pallas kernels, final(): pl.pallas_call(lambda *refs: final_kernel(groups, *refs), out_shape=out,...  6.42 us
    pallas_call x2, Pallas kernels, arrange(): pl.pallas_call(arrange_kernel, out_shape=jax.ShapeDtypeStruct((count, 128...  6.2 us
    ppermute x2, starting transfers between devices, passed_along(): return lax.ppermute(value, AXES, pairs)  5.14 us
    pallas_call x1, Pallas kernels, serve(): pl.pallas_call(lambda *refs: serve_kernel(first, *refs), out_shape=jax.Sh...  4.8 us
    pallas_call x1, Pallas kernels, body(): pl.pallas_call(multipole_kernel, out_shape=jax.ShapeDtypeStruct((members,...  3.63 us
  transfers between devices with their start and end apart: 5, of which 3 were waited for; matrix products, arithmetic and copies ran while one was open for 3% of the time, Pallas kernels for 35%

profile of v3, /device:TPU:1, one launch (start us, length us, event | category | flops | bytes accessed | tf_op | source)
XLA Modules:
  0.0 108.8 jit_solution(16223197787489077325)
XLA Ops:
  0.0 0.0 copy-start.3
  0.0 0.0 copy-start.9
  0.0 0.0 copy-start.11
  0.0 2.0 %requests.1 = (bf16[16,16,256]{2,1,0:T(8,128)(2,1)}, s32[8,320]{1,0:T(8,128)}) custom-call(s32[8,32]{1,0:T(8,128)} %bitcast.13, s32[8,32]{1,0:T(8,128)} %bitcast.14, s32[8,8]{1,0:T(8,128)} %own_upper.1, s32[8,8]{1,0:T(8,128)} %loc_upper.1), custom_call_target="tpu_custom_call" | custom-call | tf_op jit(solution)/shard_map/requests/pallas_call | solution.py:386
  2.0 8.6 %all-to-all-start.1 = ((bf16[16,16,256]{2,1,0:T(8,128)(2,1)}), bf16[16,16,256]{2,1,0:T(8,128)(2,1)S(1)}, u32[]{:S(2)}, u32[]{:S(2)}) async-start(bf16[16,16,256]{2,1,0:T(8,128)(2,1)} %get-tuple-element.70), calls=%async_computation.1 | async-start | bytes 262144 | tf_op jit(solution)/shard_map/all_to_all | solution.py:358
  10.6 0.1 pad.5.clone
  10.7 3.6 %multipoles.1 = bf16[8,80,256]{2,1,0:T(8,128)(2,1)} custom-call(bf16[64,8192]{1,0:T(8,128)(2,1)} %density.1, bf16[64,8192]{1,0:T(8,128)(2,1)} %basis.1, bf16[32,4096]{1,0:T(8,128)(2,1)} %up_ref.1), custom_call_target="tpu_custom_call" | custom-call | tf_op jit(solution)/shard_map/multipoles/pallas_call | solution.py:397
  14.3 0.0 copy-start.6
  14.3 3.1 %all-to-all-done.1 = bf16[16,16,256]{2,1,0:T(8,128)(2,1)S(1)} async-done(((bf16[16,16,256]{2,1,0:T(8,128)(2,1)}), bf16[16,16,256]{2,1,0:T(8,128)(2,1)S(1)}, u32[]{:S(2)}, u32[]{:S(2)}) %all-to-all-start.1) | async-done | bytes 131104 | tf_op jit(solution)/shard_map/all_to_all | solution.py:358
  17.5 0.0 copy-done.11
  17.5 0.0 copy-done.3
  17.5 0.0 copy-done.9
  17.5 0.3 maximum_maximum_fusion.own
  17.8 0.0 copy-start.7
  17.8 0.6 collective-permute-start
  18.5 4.5 %collective-permute-start.1 = (bf16[72,8192]{1,0:T(8,128)(2,1)S(1)}, bf16[72,8192]{1,0:T(8,128)(2,1)}, u32[]{:S(2)}, u32[]{:S(2)}) collective-permute-start(bf16[72,8192]{1,0:T(8,128)(2,1)S(1)} %maximum_maximum_fusion.own), channel_id=1, source_target_pairs={{0,127},{1,0},{2,1},{3,2},{4,3},{5,4},{6,5},{7,6},{8,7},{9,8},{10,... | collective-permute-start | bytes 3538952 | tf_op jit(solution)/shard_map/ppermute | solution.py:30
  23.0 0.0 copy-done.6
  23.0 0.8 pad_maximum_fusion
  23.8 7.5 %all-to-all-start.2 = ((bf16[8,96,256]{2,1,0:T(8,128)(2,1)}), bf16[8,96,256]{2,1,0:T(8,128)(2,1)S(1)}, u32[]{:S(2)}, u32[]{:S(2)}) async-start(bf16[8,96,256]{2,1,0:T(8,128)(2,1)} %pad_maximum_fusion), calls=%async_computation.2 | async-start | bytes 786432 | tf_op jit(solution)/shard_map/all_to_all | solution.py:358
  31.4 0.6 pad_add_fusion.first
  32.0 0.0 copy-start.8
  32.0 4.2 %arrange.2 = bf16[32,128,256]{2,1,0:T(8,128)(2,1)} custom-call(bf16[32,8,4096]{2,1,0:T(8,128)(2,1)} %couple), custom_call_target="tpu_custom_call" | custom-call | tf_op jit(solution)/shard_map/arrange/pallas_call | solution.py:163
  36.2 0.0 copy-done.7
  36.2 2.0 %arrange.3 = bf16[8,128,256]{2,1,0:T(8,128)(2,1)} custom-call(bf16[8,8,4096]{2,1,0:T(8,128)(2,1)} %couple.1), custom_call_target="tpu_custom_call" | custom-call | tf_op jit(solution)/shard_map/arrange/pallas_call | solution.py:163
  38.2 0.0 copy-done.8
  38.2 0.5 reshape.7
  38.8 1.0 copy.18
  39.8 4.2 %all-to-all-done.2.refs_0_ = bf16[8,96,256]{2,1,0:T(8,128)(2,1)S(1)} async-done(((bf16[8,96,256]{2,1,0:T(8,128)(2,1)}), bf16[8,96,256]{2,1,0:T(8,128)(2,1)S(1)}, u32[]{:S(2)}, u32[]{:S(2)}) %all-to-all-start.2) | async-done | bytes 393248 | tf_op jit(solution)/shard_map/all_to_all | solution.py:358
  44.0 4.8 %serve.3 = bf16[128,56,256]{2,1,0:T(8,128)(2,1)} custom-call(bf16[8,96,256]{2,1,0:T(8,128)(2,1)S(1)} %all-to-all-done.2.refs_0_), custom_call_target="tpu_custom_call" | custom-call | tf_op jit(solution)/shard_map/serve/pallas_call | solution.py:139
  48.8 0.7 slice_reduce_fusion
  50.1 0.0 copy-done.4
  50.1 6.1 %all-to-all-start.3 = ((bf16[128,56,256]{2,1,0:T(8,128)(2,1)}), bf16[128,56,256]{2,1,0:T(8,128)(2,1)}, u32[]{:S(2)}, u32[]{:S(2)}) async-start(bf16[128,56,256]{2,1,0:T(8,128)(2,1)} %serve.3), calls=%async_computation.3 | async-start | bytes 7340032 | tf_op jit(solution)/shard_map/all_to_all | solution.py:358
  56.2 0.0 collective-permute-done.before
  56.2 0.0 collective-permute-done.1.following
  56.2 0.0 copy-start
  56.2 0.0 copy-start.1
  56.3 0.0 copy-start.2
  56.3 0.0 copy-start.5
  56.3 0.0 copy-start.10
  56.3 23.8 %near.1 = f32[32,64,256]{2,1,0:T(8,128)} custom-call(s32[9,32]{1,0:T(8,128)} %bitcast.15, s32[2]{0:T(128)} %pad_add_fusion.first, bf16[72,8192]{1,0:T(8,128)(2,1)} %collective-permute-done.before, bf16[72,8192]{1,0:T(8,128)(2,1)} %copy-done.7, bf16[72,8192]{1,0:T(8,128)(2,1)} %collective-permute-done.1.following), custom_call_target="tpu_custom_call" | custom-call | flops 483183820800 | bytes 6291456 | tf_op jit(solution)/shard_map/near/pallas_call | solution.py:235
  80.1 22.0 %all-to-all-done.3 = bf16[128,56,256]{2,1,0:T(8,128)(2,1)} async-done(((bf16[128,56,256]{2,1,0:T(8,128)(2,1)}), bf16[128,56,256]{2,1,0:T(8,128)(2,1)}, u32[]{:S(2)}, u32[]{:S(2)}) %all-to-all-start.3) | async-done | bytes 3670048 | tf_op jit(solution)/shard_map/all_to_all | solution.py:358
  102.0 0.0 copy-done
  102.0 0.0 copy-done.1
  102.0 0.0 copy-done.2
  102.0 0.0 copy-done.5
  102.0 0.0 copy-done.10
  102.1 6.6 %conditional.1 = (bf16[64,8192]{1,0:T(8,128)(2,1)}) conditional(s32[]{:T(128)} %convert_element_type.4, (s32[8,320]{1,0:T(8,128)S(1)}, bf16[128,56,256]{2,1,0:T(8,128)(2,1)}, bf16[8,128,256]{2,1,0:T(8,128)(2,1)S(1)}, bf16[8,256,64]{2,1,0:T(8,128)(2,1)S(1)}, bf16[32,128,256]{2,1,0:T(8,128)(2,1)S(1)}, /*index=5*/bf16[64,8192]{1,0:T(8,128)(2,1)}, ...), branch_computations={%region_1.0_spmd, %region_2.0_spmd} | conditional | bytes 3145736 | solution.py:448
  102.2 6.4 %far.2 = bf16[64,8192]{1,0:T(8,128)(2,1)} custom-call(s32[8,320]{1,0:T(8,128)S(1)} %get-tuple-element.38.refs_0_, bf16[128,56,256]{2,1,0:T(8,128)(2,1)} %get-tuple-element.39.refs_1_, bf16[8,128,256]{2,1,0:T(8,128)(2,1)S(1)} %get-tuple-element.40.refs_2_, bf16[8,256,64]{2,1,0:T(8,128)(2,1)S(1)} %get-tuple-element.41.refs_3_, ...), custom_call_target="tpu_custom_call" | custom-call | tf_op jit(solution)/shard_map/cond/branch_0_fun/far/pallas_call | solution.py:339
  (6 shorter events, 0.0 us)
Async XLA Ops:
  0.0 17.5 %copy-start.3 = (bf16[64,8192]{1,0:T(8,128)(2,1)S(1)}, bf16[64,8192]{1,0:T(8,128)(2,1)}, u32[]{:S(2)}) copy-start(bf16[64,8192]{1,0:T(8,128)(2,1)} %density.1) | copy-start | bytes 3145732
  0.0 17.5 %copy-start.9 = (bf16[3,8192]{1,0:T(4,128)(2,1)S(1)}, bf16[3,8192]{1,0:T(4,128)(2,1)}, u32[]{:S(2)}) copy-start(bf16[3,8192]{1,0:T(4,128)(2,1)} %param.17) | copy-start | bytes 147460
  0.0 17.5 %copy-start.11 = (bf16[8192]{0:T(1024)(128)(2,1)S(1)}, bf16[8192]{0:T(1024)(128)(2,1)}, u32[]{:S(2)}) copy-start(bf16[8192]{0:T(1024)(128)(2,1)} %param.18) | copy-start | bytes 49156
  2.0 15.5 %all-to-all-start.1 = ((bf16[16,16,256]{2,1,0:T(8,128)(2,1)}), bf16[16,16,256]{2,1,0:T(8,128)(2,1)S(1)}, u32[]{:S(2)}, u32[]{:S(2)}) async-start(bf16[16,16,256]{2,1,0:T(8,128)(2,1)} %get-tuple-element.70), calls=%async_computation.1 | async-start | bytes 262144 | tf_op jit(solution)/shard_map/all_to_all | solution.py:358
  14.3 8.7 %copy-start.6 = (bf16[8,80,256]{2,1,0:T(8,128)(2,1)S(1)}, bf16[8,80,256]{2,1,0:T(8,128)(2,1)}, u32[]{:S(2)}) copy-start(bf16[8,80,256]{2,1,0:T(8,128)(2,1)} %multipoles.1) | copy-start | bytes 983044
  17.8 18.3 %copy-start.7 = (bf16[72,8192]{1,0:T(8,128)(2,1)}, bf16[72,8192]{1,0:T(8,128)(2,1)S(1)}, u32[]{:S(2)}) copy-start(bf16[72,8192]{1,0:T(8,128)(2,1)S(1)} %maximum_maximum_fusion.own) | copy-start | bytes 3538948
  17.8 38.4 %collective-permute-start = (bf16[72,8192]{1,0:T(8,128)(2,1)S(1)}, bf16[72,8192]{1,0:T(8,128)(2,1)}, u32[]{:S(2)}, u32[]{:S(2)}) collective-permute-start(bf16[72,8192]{1,0:T(8,128)(2,1)S(1)} %maximum_maximum_fusion.own), channel_id=1, source_target_pairs={{0,1},{1,2},{2,3},{3,4},{4,5},{5,6},{6,7},{7,8},{8,9},{9,10},{10,1... | collective-permute-start | bytes 3538952 | tf_op jit(solution)/shard_map/ppermute | solution.py:30
  18.5 37.7 %collective-permute-start.1 = (bf16[72,8192]{1,0:T(8,128)(2,1)S(1)}, bf16[72,8192]{1,0:T(8,128)(2,1)}, u32[]{:S(2)}, u32[]{:S(2)}) collective-permute-start(bf16[72,8192]{1,0:T(8,128)(2,1)S(1)} %maximum_maximum_fusion.own), channel_id=1, source_target_pairs={{0,127},{1,0},{2,1},{3,2},{4,3},{5,4},{6,5},{7,6},{8,7},{9,8},{10,... | collective-permute-start | bytes 3538952 | tf_op jit(solution)/shard_map/ppermute | solution.py:30
  23.8 20.2 %all-to-all-start.2 = ((bf16[8,96,256]{2,1,0:T(8,128)(2,1)}), bf16[8,96,256]{2,1,0:T(8,128)(2,1)S(1)}, u32[]{:S(2)}, u32[]{:S(2)}) async-start(bf16[8,96,256]{2,1,0:T(8,128)(2,1)} %pad_maximum_fusion), calls=%async_computation.2 | async-start | bytes 786432 | tf_op jit(solution)/shard_map/all_to_all | solution.py:358
  32.0 6.2 %copy-start.8 = (bf16[32,4096]{1,0:T(8,128)(2,1)S(1)}, bf16[32,4096]{1,0:T(8,128)(2,1)}, u32[]{:S(2)}) copy-start(bf16[32,4096]{1,0:T(8,128)(2,1)} %param.22) | copy-start | bytes 786436
  44.0 6.1 %copy-start.4 = (bf16[8,96,256]{2,1,0:T(8,128)(2,1)}, bf16[8,96,256]{2,1,0:T(8,128)(2,1)S(1)}, u32[]{:S(2)}) copy-start(bf16[8,96,256]{2,1,0:T(8,128)(2,1)S(1)} %all-to-all-done.2.refs_0_) | copy-start | bytes 1179652
  50.1 51.9 %all-to-all-start.3 = ((bf16[128,56,256]{2,1,0:T(8,128)(2,1)}), bf16[128,56,256]{2,1,0:T(8,128)(2,1)}, u32[]{:S(2)}, u32[]{:S(2)}) async-start(bf16[128,56,256]{2,1,0:T(8,128)(2,1)} %serve.3), calls=%async_computation.3 | async-start | bytes 7340032 | tf_op jit(solution)/shard_map/all_to_all | solution.py:358
  56.2 45.8 %copy-start = (bf16[32,128,256]{2,1,0:T(8,128)(2,1)S(1)}, bf16[32,128,256]{2,1,0:T(8,128)(2,1)}, u32[]{:S(2)}) copy-start(bf16[32,128,256]{2,1,0:T(8,128)(2,1)} %arrange.2) | copy-start | bytes 6291460
  56.2 45.8 %copy-start.1 = (bf16[8,128,256]{2,1,0:T(8,128)(2,1)S(1)}, bf16[8,128,256]{2,1,0:T(8,128)(2,1)}, u32[]{:S(2)}) copy-start(bf16[8,128,256]{2,1,0:T(8,128)(2,1)} %arrange.3) | copy-start | bytes 1572868
  56.3 45.8 %copy-start.2 = (bf16[8,4,64,64]{2,3,1,0:T(8,128)(2,1)S(1)}, bf16[8,4,64,64]{2,3,1,0:T(8,128)(2,1)}, u32[]{:S(2)}) copy-start(bf16[8,4,64,64]{2,3,1,0:T(8,128)(2,1)} %copy.18) | copy-start | bytes 786436
  56.3 45.8 %copy-start.5 = (bf16[8,96,256]{2,1,0:T(8,128)(2,1)S(1)}, bf16[8,96,256]{2,1,0:T(8,128)(2,1)}, u32[]{:S(2)}) copy-start(bf16[8,96,256]{2,1,0:T(8,128)(2,1)} %copy-done.4) | copy-start | bytes 1179652
  56.3 45.8 %copy-start.10 = (s32[8,320]{1,0:T(8,128)S(1)}, s32[8,320]{1,0:T(8,128)}, u32[]{:S(2)}) copy-start(s32[8,320]{1,0:T(8,128)} %get-tuple-element.81) | copy-start | bytes 30724

commit v4 on v3

--- a/solution.py
+++ b/solution.py
@@ -24,10 +24,10 @@
     return lax.dot_general(a, b, dims, preferred_element_type=F32)
 
 
-def passed_along(value, steps):
+def swapped(value, first):
     count = lax.axis_size(AXES)
-    pairs = [(source, (source + steps) % count) for source in range(count)]
-    return lax.ppermute(value, AXES, pairs)
+    pairs = [(one, (one + 1) % count) for one in range(first, count, 2)]
+    return lax.ppermute(value, AXES, pairs + [(b, a) for a, b in pairs])
 
 
 def iota(shape, dim):
@@ -177,22 +177,23 @@
     return high, middle, value - high - middle
 
 
-def near_kernel(listed, first, before, own, following, out_ref, window, sources, targets, kern):
+def near_kernel(listed, first, one_side, own, other_side, out_ref, window, sources, targets, kern):
     leaves, rows, size = out_ref.shape
     near = listed.shape[0]
     wide = own.shape[1]
     total = first[1]
     one = jnp.ones((3, wide), F32)
     zero = jnp.zeros((6, wide), F32)
-    for place, ref in enumerate((before, own, following)):
-        cut = slice(place * wide, (place + 1) * wide)
+    odd = first[2]
+    for ref, place in ((one_side, 2 - 2 * odd), (own, 1), (other_side, 2 * odd)):
+        cut = pl.ds(pl.multiple_of(place * wide, wide), wide)
         window[:, cut] = ref[:rows]
         y = ref[rows:].astype(F32)
         square = y[0:1] * y[0:1] + y[1:2] * y[1:2] + y[2:3] * y[2:3]
         sources[cut] = jnp.transpose(
             jnp.concatenate([-2.0 * y[0:3], one, *pieces(square + SOFTEN), y[3:4], zero], axis=0)
         ).astype(BF16)
-        if place == 1:
+        if ref is own:
             targets[...] = jnp.concatenate(
                 [y[0:3], *pieces(square), one, zero, zero[:1]], axis=0
             ).astype(BF16)
@@ -228,7 +229,7 @@
     lax.fori_loop(0, leaves // 2, two, 0)
 
 
-def near_field(listed, first, before, own, following, leaves, rows):
+def near_field(listed, first, one_side, own, other_side, leaves, rows):
     wide = own.shape[1]
     size = wide // leaves
     near = listed.shape[0]
@@ -250,7 +251,7 @@
             transcendentals=leaves * near * size * size,
         ),
         name="near",
-    )(listed, first, before, own, following)
+    )(listed, first, one_side, own, other_side)
 
 
 def final_kernel(groups, places, *refs):
@@ -386,7 +387,7 @@
     asks, places = pl.pallas_call(
         request_kernel,
         out_shape=(
-            jax.ShapeDtypeStruct((groups, 16, 256), BF16),
+            jax.ShapeDtypeStruct((groups, 8, 256), BF16),
             jax.ShapeDtypeStruct((8, rows * fan), jnp.int32),
         ),
         in_specs=[VMEM] * 4,
@@ -414,8 +415,7 @@
     own = jnp.concatenate(
         [density, points, weights[None], jnp.zeros((4, density.shape[1]), BF16)], axis=0
     )
-    before = passed_along(own, 1)
-    following = passed_along(own, -1)
+    one_side, other_side = swapped(own, 0), swapped(own, 1)
     asked = jnp.broadcast_to(asked[None, :, 0, :], (members, groups, asked.shape[2]))
     slices = jnp.concatenate([slices, asked], axis=1)
 
@@ -430,13 +430,15 @@
         .transpose(0, 1, 3, 2)
         .reshape(uppers, 4 * rank, rank)
     )
-    first = jnp.stack([lax.axis_index(AXES) * leaves, jnp.int32(leaves * devices)])
+    place = lax.axis_index(AXES)
+    first = jnp.stack([place * leaves, jnp.int32(leaves * devices), place % 2])
     slices, leaf_mats, upper_mats, down, first = lax.optimization_barrier(
         (slices, leaf_mats, upper_mats, down, first)
     )
     replies = exchange(serve(slices, groups, 0, 2 * SENT), AXES)
-    near = near_field(near_list.T, first, before, own, following, leaves, vectors)
-    most = jnp.max(slices[:, 2 * rows :, 127].astype(F32))
+    near = near_field(near_list.T, first, one_side, own, other_side, leaves, vectors)
+    near, late = lax.optimization_barrier((near, slices[:, 2 * rows :]))
+    most = jnp.max(late[:, :, 127].astype(F32))
 
     def finish(*received):
         return final(groups, places, received, upper_mats, down, leaf_mats, target_basis, near)

time: 109 us -> 106 us (0.972)
  waiting for transfers between devices: 29.3 us -> 26.6 us
    all_to_all x3, waiting for transfers between devices: 29.3 us -> 26.6 us  [exchange(): return lax.all_to_all(value, axes, split_axis=0, concat_axis=0, tiled=True)]
    ppermute x2, starting transfers between devices: 5.14 us -> 3.56 us  [swapped(): return lax.ppermute(value, AXES, pairs + [(b, a) for a, b in pairs])]
  transfers between devices with their start and end apart: 5 -> 5, of which waited for: 3 -> 3; matrix products, arithmetic and copies ran while one was open for 3% -> 4% of each run, Pallas kernels for 35% -> 37%
where the time goes in v4:
time: 106 us; the launch traced here: 105 us
  Pallas kernels  46.9 us (44%)
  waiting for transfers between devices  26.6 us (25%)
  starting transfers between devices  26.5 us (25%)
  other arithmetic  2.4 us (2%)
  local copies, waits for them, and re-layouts  1.74 us (2%)
    all_to_all x3, waiting for transfers between devices, exchange(): return lax.all_to_all(value, axes, split_axis=0, concat_axis=0, tiled=True)  26.6 us
    pallas_call x1, Pallas kernels, near_field(): pl.pallas_call(near_kernel, out_shape=jax.ShapeDtypeStruct((leaves, rows,...  23.9 us
    all_to_all x3, starting transfers between devices, exchange(): return lax.all_to_all(value, axes, split_axis=0, concat_axis=0, tiled=True)  23 us
    pallas_call x1, Pallas kernels, final(): pl.pallas_call(lambda *refs: final_kernel(groups, *refs), out_shape=out,...  6.42 us
    pallas_call x2, Pallas kernels, arrange(): pl.pallas_call(arrange_kernel, out_shape=jax.ShapeDtypeStruct((count, 128...  6.18 us
    pallas_call x1, Pallas kernels, serve(): pl.pallas_call(lambda *refs: serve_kernel(first, *refs), out_shape=jax.Sh...  4.8 us
    pallas_call x1, Pallas kernels, body(): pl.pallas_call(multipole_kernel, out_shape=jax.ShapeDtypeStruct((members,...  3.63 us
    ppermute x2, starting transfers between devices, swapped(): return lax.ppermute(value, AXES, pairs + [(b, a) for a, b in pairs])  3.56 us
  transfers between devices with their start and end apart: 5, of which 3 were waited for; matrix products, arithmetic and copies ran while one was open for 4% of the time, Pallas kernels for 37%

profile of v4, /device:TPU:1, one launch (start us, length us, event | category | flops | bytes accessed | tf_op | source)
XLA Modules:
  0.0 105.3 jit_solution(14249153059409856707)
XLA Ops:
  0.0 0.0 copy-start.3
  0.0 0.0 copy-start.10
  0.0 0.0 copy-start.8
  0.0 2.0 %requests.1 = (bf16[16,8,256]{2,1,0:T(8,128)(2,1)}, s32[8,320]{1,0:T(8,128)}) custom-call(s32[8,32]{1,0:T(8,128)} %bitcast.14, s32[8,32]{1,0:T(8,128)} %bitcast.15, s32[8,8]{1,0:T(8,128)} %own_upper.1, s32[8,8]{1,0:T(8,128)} %loc_upper.1), custom_call_target="tpu_custom_call" | custom-call | tf_op jit(solution)/shard_map/requests/pallas_call | solution.py:387
  2.0 8.6 %all-to-all-start.1 = ((bf16[16,8,256]{2,1,0:T(8,128)(2,1)}), bf16[16,8,256]{2,1,0:T(8,128)(2,1)S(1)}, u32[]{:S(2)}, u32[]{:S(2)}) async-start(bf16[16,8,256]{2,1,0:T(8,128)(2,1)} %get-tuple-element.72), calls=%async_computation.1 | async-start | bytes 131072 | tf_op jit(solution)/shard_map/all_to_all | solution.py:359
  10.6 0.1 pad.6.clone
  10.7 3.6 %multipoles.1 = bf16[8,80,256]{2,1,0:T(8,128)(2,1)} custom-call(bf16[64,8192]{1,0:T(8,128)(2,1)} %density.1, bf16[64,8192]{1,0:T(8,128)(2,1)} %basis.1, bf16[32,4096]{1,0:T(8,128)(2,1)} %up_ref.1), custom_call_target="tpu_custom_call" | custom-call | tf_op jit(solution)/shard_map/multipoles/pallas_call | solution.py:398
  14.3 0.0 copy-start.5
  14.3 2.8 %all-to-all-done.1 = bf16[16,8,256]{2,1,0:T(8,128)(2,1)S(1)} async-done(((bf16[16,8,256]{2,1,0:T(8,128)(2,1)}), bf16[16,8,256]{2,1,0:T(8,128)(2,1)S(1)}, u32[]{:S(2)}, u32[]{:S(2)}) %all-to-all-start.1) | async-done | bytes 65568 | tf_op jit(solution)/shard_map/all_to_all | solution.py:359
  17.1 0.0 copy-done.10
  17.1 0.0 copy-done.3
  17.2 0.0 copy-done.8
  17.2 0.0 copy-start.7
  17.2 0.3 maximum_maximum_fusion.own
  17.5 0.0 copy-start.6
  17.5 3.6 %collective-permute-start.1 = (bf16[72,8192]{1,0:T(8,128)(2,1)S(1)}, bf16[72,8192]{1,0:T(8,128)(2,1)}, u32[]{:S(2)}, u32[]{:S(2)}) collective-permute-start(bf16[72,8192]{1,0:T(8,128)(2,1)S(1)} %maximum_maximum_fusion.own), channel_id=1, source_target_pairs={{1,2},{3,4},{5,6},{7,8},{9,10},{11,12},{13,14},{15,16},{17,18},{19... | collective-permute-start | bytes 3538952 | tf_op jit(solution)/shard_map/ppermute | solution.py:30
  21.0 0.0 collective-permute-start
  21.1 0.0 copy-done.5
  21.1 0.8 pad_maximum_fusion
  21.9 4.4 %all-to-all-start.2 = ((bf16[8,96,256]{2,1,0:T(8,128)(2,1)}), bf16[8,96,256]{2,1,0:T(8,128)(2,1)S(1)}, u32[]{:S(2)}, u32[]{:S(2)}) async-start(bf16[8,96,256]{2,1,0:T(8,128)(2,1)} %pad_maximum_fusion), calls=%async_computation.2 | async-start | bytes 786432 | tf_op jit(solution)/shard_map/all_to_all | solution.py:359
  26.3 0.7 pad_add_fusion.first
  26.9 2.0 %arrange.3 = bf16[8,128,256]{2,1,0:T(8,128)(2,1)} custom-call(bf16[8,8,4096]{2,1,0:T(8,128)(2,1)} %couple.1), custom_call_target="tpu_custom_call" | custom-call | tf_op jit(solution)/shard_map/arrange/pallas_call | solution.py:163
  29.0 0.0 copy-done.7
  29.0 0.5 reshape.7
  29.5 1.0 copy.18
  30.6 0.0 copy-done.6
  30.6 4.1 %arrange.2 = bf16[32,128,256]{2,1,0:T(8,128)(2,1)} custom-call(bf16[32,8,4096]{2,1,0:T(8,128)(2,1)} %couple), custom_call_target="tpu_custom_call" | custom-call | tf_op jit(solution)/shard_map/arrange/pallas_call | solution.py:163
  34.7 3.2 %all-to-all-done.2.refs_0_ = bf16[8,96,256]{2,1,0:T(8,128)(2,1)S(1)} async-done(((bf16[8,96,256]{2,1,0:T(8,128)(2,1)}), bf16[8,96,256]{2,1,0:T(8,128)(2,1)S(1)}, u32[]{:S(2)}, u32[]{:S(2)}) %all-to-all-start.2) | async-done | bytes 393248 | tf_op jit(solution)/shard_map/all_to_all | solution.py:359
  37.9 4.8 %serve.3 = bf16[128,56,256]{2,1,0:T(8,128)(2,1)} custom-call(bf16[8,96,256]{2,1,0:T(8,128)(2,1)S(1)} %all-to-all-done.2.refs_0_), custom_call_target="tpu_custom_call" | custom-call | tf_op jit(solution)/shard_map/serve/pallas_call | solution.py:139
  42.7 0.0 copy-done.4
  42.7 10.0 %all-to-all-start.3 = ((bf16[128,56,256]{2,1,0:T(8,128)(2,1)}), bf16[128,56,256]{2,1,0:T(8,128)(2,1)}, u32[]{:S(2)}, u32[]{:S(2)}) async-start(bf16[128,56,256]{2,1,0:T(8,128)(2,1)} %serve.3), calls=%async_computation.3 | async-start | bytes 7340032 | tf_op jit(solution)/shard_map/all_to_all | solution.py:359
  52.7 0.0 collective-permute-done.1.other_side
  52.7 0.0 collective-permute-done.one_side
  52.7 0.0 slice-start
  52.7 0.0 copy-start
  52.7 0.0 copy-start.1
  52.7 0.0 copy-start.2
  52.7 0.0 copy-start.9
  52.7 23.9 %near.1 = f32[32,64,256]{2,1,0:T(8,128)} custom-call(s32[9,32]{1,0:T(8,128)} %bitcast.16, s32[3]{0:T(128)} %pad_add_fusion.first, bf16[72,8192]{1,0:T(8,128)(2,1)} %collective-permute-done.one_side, bf16[72,8192]{1,0:T(8,128)(2,1)} %copy-done.6, bf16[72,8192]{1,0:T(8,128)(2,1)} %collective-permute-done.1.other_side), custom_call_target="tpu_custom_call" | custom-call | flops 483183820800 | bytes 6291456 | tf_op jit(solution)/shard_map/near/pallas_call | solution.py:236
  76.6 0.0 slice-done
  76.6 0.7 slice_reduce_fusion
  77.9 20.6 %all-to-all-done.3 = bf16[128,56,256]{2,1,0:T(8,128)(2,1)} async-done(((bf16[128,56,256]{2,1,0:T(8,128)(2,1)}), bf16[128,56,256]{2,1,0:T(8,128)(2,1)}, u32[]{:S(2)}, u32[]{:S(2)}) %all-to-all-start.3) | async-done | bytes 3670048 | tf_op jit(solution)/shard_map/all_to_all | solution.py:359
  98.5 0.0 copy-done
  98.5 0.0 copy-done.1
  98.5 0.0 copy-done.2
  98.5 0.0 copy-done.9
  98.5 6.6 %conditional.1 = (bf16[64,8192]{1,0:T(8,128)(2,1)}) conditional(s32[]{:T(128)} %convert_element_type.4, (s32[8,320]{1,0:T(8,128)S(1)}, bf16[128,56,256]{2,1,0:T(8,128)(2,1)}, bf16[8,128,256]{2,1,0:T(8,128)(2,1)S(1)}, bf16[8,256,64]{2,1,0:T(8,128)(2,1)S(1)}, bf16[32,128,256]{2,1,0:T(8,128)(2,1)S(1)}, /*index=5*/bf16[64,8192]{1,0:T(8,128)(2,1)}, ...), branch_computations={%region_1.2_spmd, %region_2.3_spmd} | conditional | bytes 3145736 | solution.py:450
  98.7 6.4 %far.2 = bf16[64,8192]{1,0:T(8,128)(2,1)} custom-call(s32[8,320]{1,0:T(8,128)S(1)} %get-tuple-element.38.refs_0_, bf16[128,56,256]{2,1,0:T(8,128)(2,1)} %get-tuple-element.39.refs_1_, bf16[8,128,256]{2,1,0:T(8,128)(2,1)S(1)} %get-tuple-element.40.refs_2_, bf16[8,256,64]{2,1,0:T(8,128)(2,1)S(1)} %get-tuple-element.41.refs_3_, ...), custom_call_target="tpu_custom_call" | custom-call | tf_op jit(solution)/shard_map/cond/branch_0_fun/far/pallas_call | solution.py:340
  (6 shorter events, 0.0 us)
Async XLA Ops:
  0.0 17.1 %copy-start.3 = (bf16[64,8192]{1,0:T(8,128)(2,1)S(1)}, bf16[64,8192]{1,0:T(8,128)(2,1)}, u32[]{:S(2)}) copy-start(bf16[64,8192]{1,0:T(8,128)(2,1)} %density.1) | copy-start | bytes 3145732
  0.0 17.1 %copy-start.10 = (bf16[8192]{0:T(1024)(128)(2,1)S(1)}, bf16[8192]{0:T(1024)(128)(2,1)}, u32[]{:S(2)}) copy-start(bf16[8192]{0:T(1024)(128)(2,1)} %param.18) | copy-start | bytes 49156
  0.0 17.2 %copy-start.8 = (bf16[3,8192]{1,0:T(4,128)(2,1)S(1)}, bf16[3,8192]{1,0:T(4,128)(2,1)}, u32[]{:S(2)}) copy-start(bf16[3,8192]{1,0:T(4,128)(2,1)} %param.17) | copy-start | bytes 147460
  2.0 15.1 %all-to-all-start.1 = ((bf16[16,8,256]{2,1,0:T(8,128)(2,1)}), bf16[16,8,256]{2,1,0:T(8,128)(2,1)S(1)}, u32[]{:S(2)}, u32[]{:S(2)}) async-start(bf16[16,8,256]{2,1,0:T(8,128)(2,1)} %get-tuple-element.72), calls=%async_computation.1 | async-start | bytes 131072 | tf_op jit(solution)/shard_map/all_to_all | solution.py:359
  14.3 6.8 %copy-start.5 = (bf16[8,80,256]{2,1,0:T(8,128)(2,1)S(1)}, bf16[8,80,256]{2,1,0:T(8,128)(2,1)}, u32[]{:S(2)}) copy-start(bf16[8,80,256]{2,1,0:T(8,128)(2,1)} %multipoles.1) | copy-start | bytes 983044
  17.2 11.8 %copy-start.7 = (bf16[32,4096]{1,0:T(8,128)(2,1)S(1)}, bf16[32,4096]{1,0:T(8,128)(2,1)}, u32[]{:S(2)}) copy-start(bf16[32,4096]{1,0:T(8,128)(2,1)} %param.22) | copy-start | bytes 786436
  17.5 13.1 %copy-start.6 = (bf16[72,8192]{1,0:T(8,128)(2,1)}, bf16[72,8192]{1,0:T(8,128)(2,1)S(1)}, u32[]{:S(2)}) copy-start(bf16[72,8192]{1,0:T(8,128)(2,1)S(1)} %maximum_maximum_fusion.own) | copy-start | bytes 3538948
  17.5 35.2 %collective-permute-start.1 = (bf16[72,8192]{1,0:T(8,128)(2,1)S(1)}, bf16[72,8192]{1,0:T(8,128)(2,1)}, u32[]{:S(2)}, u32[]{:S(2)}) collective-permute-start(bf16[72,8192]{1,0:T(8,128)(2,1)S(1)} %maximum_maximum_fusion.own), channel_id=1, source_target_pairs={{1,2},{3,4},{5,6},{7,8},{9,10},{11,12},{13,14},{15,16},{17,18},{19... | collective-permute-start | bytes 3538952 | tf_op jit(solution)/shard_map/ppermute | solution.py:30
  21.0 31.6 %collective-permute-start = (bf16[72,8192]{1,0:T(8,128)(2,1)S(1)}, bf16[72,8192]{1,0:T(8,128)(2,1)}, u32[]{:S(2)}, u32[]{:S(2)}) collective-permute-start(bf16[72,8192]{1,0:T(8,128)(2,1)S(1)} %maximum_maximum_fusion.own), channel_id=1, source_target_pairs={{0,1},{2,3},{4,5},{6,7},{8,9},{10,11},{12,13},{14,15},{16,17},{18,... | collective-permute-start | bytes 3538952 | tf_op jit(solution)/shard_map/ppermute | solution.py:30
  21.9 16.0 %all-to-all-start.2 = ((bf16[8,96,256]{2,1,0:T(8,128)(2,1)}), bf16[8,96,256]{2,1,0:T(8,128)(2,1)S(1)}, u32[]{:S(2)}, u32[]{:S(2)}) async-start(bf16[8,96,256]{2,1,0:T(8,128)(2,1)} %pad_maximum_fusion), calls=%async_computation.2 | async-start | bytes 786432 | tf_op jit(solution)/shard_map/all_to_all | solution.py:359
  37.9 4.8 %copy-start.4 = (bf16[8,96,256]{2,1,0:T(8,128)(2,1)}, bf16[8,96,256]{2,1,0:T(8,128)(2,1)S(1)}, u32[]{:S(2)}) copy-start(bf16[8,96,256]{2,1,0:T(8,128)(2,1)S(1)} %all-to-all-done.2.refs_0_) | copy-start | bytes 1179652
  42.7 55.8 %all-to-all-start.3 = ((bf16[128,56,256]{2,1,0:T(8,128)(2,1)}), bf16[128,56,256]{2,1,0:T(8,128)(2,1)}, u32[]{:S(2)}, u32[]{:S(2)}) async-start(bf16[128,56,256]{2,1,0:T(8,128)(2,1)} %serve.3), calls=%async_computation.3 | async-start | bytes 7340032 | tf_op jit(solution)/shard_map/all_to_all | solution.py:359
  52.7 23.9 %slice-start = ((bf16[8,96,256]{2,1,0:T(8,128)(2,1)}), bf16[8,16,256]{2,1,0:T(8,128)(2,1)S(1)}, s32[]{:S(2)}) async-start(bf16[8,96,256]{2,1,0:T(8,128)(2,1)} %copy-done.4), calls=%async_computation.4 | async-start | bytes 131072 | tf_op jit(solution)/shard_map/slice | solution.py:440
  52.7 45.8 %copy-start = (bf16[32,128,256]{2,1,0:T(8,128)(2,1)S(1)}, bf16[32,128,256]{2,1,0:T(8,128)(2,1)}, u32[]{:S(2)}) copy-start(bf16[32,128,256]{2,1,0:T(8,128)(2,1)} %arrange.2) | copy-start | bytes 6291460
  52.7 45.8 %copy-start.1 = (bf16[8,128,256]{2,1,0:T(8,128)(2,1)S(1)}, bf16[8,128,256]{2,1,0:T(8,128)(2,1)}, u32[]{:S(2)}) copy-start(bf16[8,128,256]{2,1,0:T(8,128)(2,1)} %arrange.3) | copy-start | bytes 1572868
  52.7 45.8 %copy-start.2 = (bf16[8,4,64,64]{2,3,1,0:T(8,128)(2,1)S(1)}, bf16[8,4,64,64]{2,3,1,0:T(8,128)(2,1)}, u32[]{:S(2)}) copy-start(bf16[8,4,64,64]{2,3,1,0:T(8,128)(2,1)} %copy.18) | copy-start | bytes 786436
  52.7 45.8 %copy-start.9 = (s32[8,320]{1,0:T(8,128)S(1)}, s32[8,320]{1,0:T(8,128)}, u32[]{:S(2)}) copy-start(s32[8,320]{1,0:T(8,128)} %get-tuple-element.86) | copy-start | bytes 30724

commit v5 on v4

--- a/solution.py
+++ b/solution.py
@@ -80,7 +80,7 @@
     leaves = up_ref.shape[0]
     rank = square.shape[1]
     half = rank // 2
-    rows = table.shape[0] // half
+    rows = out_ref.shape[1] // 2
     size = density.shape[1] // leaves
     for leaf in range(leaves):
         cut = slice(leaf * size, (leaf + 1) * size)
@@ -401,9 +401,9 @@
         in_specs=[VMEM] * 3,
         out_specs=VMEM,
         scratch_shapes=[
-            pltpu.VMEM((rows * rank, vectors), F32),
-            pltpu.VMEM((rows * half, 2 * vectors), F32),
-            pltpu.VMEM((leaves * half, 2 * rank), F32),
+            pltpu.VMEM((rows * rank + 8, vectors), F32),
+            pltpu.VMEM((rows * half + half, 2 * vectors), F32),
+            pltpu.VMEM((leaves * half + half, 2 * rank), F32),
         ],
         compiler_params=pltpu.CompilerParams(vmem_limit_bytes=ROOM),
         name="multipoles",

time: 106 us -> 106 us (level)
  no operation moved by 1% of the time
where the time goes in v5:
time: 106 us; the launch traced here: 105 us
  Pallas kernels  46.9 us (44%)
  starting transfers between devices  26.6 us (25%)
  waiting for transfers between devices  26.6 us (25%)
  other arithmetic  2.4 us (2%)
  local copies, waits for them, and re-layouts  1.74 us (2%)
    all_to_all x3, waiting for transfers between devices, exchange(): return lax.all_to_all(value, axes, split_axis=0, concat_axis=0, tiled=True)  26.6 us
    pallas_call x1, Pallas kernels, near_field(): pl.pallas_call(near_kernel, out_shape=jax.ShapeDtypeStruct((leaves, rows,...  23.9 us
    all_to_all x3, starting transfers between devices, exchange(): return lax.all_to_all(value, axes, split_axis=0, concat_axis=0, tiled=True)  23 us
    pallas_call x1, Pallas kernels, final(): pl.pallas_call(lambda *refs: final_kernel(groups, *refs), out_shape=out,...  6.42 us
    pallas_call x2, Pallas kernels, arrange(): pl.pallas_call(arrange_kernel, out_shape=jax.ShapeDtypeStruct((count, 128...  6.18 us
    pallas_call x1, Pallas kernels, serve(): pl.pallas_call(lambda *refs: serve_kernel(first, *refs), out_shape=jax.Sh...  4.8 us
    pallas_call x1, Pallas kernels, body(): pl.pallas_call(multipole_kernel, out_shape=jax.ShapeDtypeStruct((members,...  3.63 us
    ppermute x2, starting transfers between devices, swapped(): return lax.ppermute(value, AXES, pairs + [(b, a) for a, b in pairs])  3.56 us
  transfers between devices with their start and end apart: 5, of which 3 were waited for; matrix products, arithmetic and copies ran while one was open for 4% of the time, Pallas kernels for 37%

profile of v5, /device:TPU:1, one launch (start us, length us, event | category | flops | bytes accessed | tf_op | source)
XLA Modules:
  0.0 105.3 jit_solution(6588177142206974199)
XLA Ops:
  0.0 0.0 copy-start.3
  0.0 0.0 copy-start.10
  0.0 0.0 copy-start.8
  0.0 2.0 %requests.1 = (bf16[16,8,256]{2,1,0:T(8,128)(2,1)}, s32[8,320]{1,0:T(8,128)}) custom-call(s32[8,32]{1,0:T(8,128)} %bitcast.14, s32[8,32]{1,0:T(8,128)} %bitcast.15, s32[8,8]{1,0:T(8,128)} %own_upper.1, s32[8,8]{1,0:T(8,128)} %loc_upper.1), custom_call_target="tpu_custom_call" | custom-call | tf_op jit(solution)/shard_map/requests/pallas_call | solution.py:387
  2.0 8.6 %all-to-all-start.1 = ((bf16[16,8,256]{2,1,0:T(8,128)(2,1)}), bf16[16,8,256]{2,1,0:T(8,128)(2,1)S(1)}, u32[]{:S(2)}, u32[]{:S(2)}) async-start(bf16[16,8,256]{2,1,0:T(8,128)(2,1)} %get-tuple-element.72), calls=%async_computation.1 | async-start | bytes 131072 | tf_op jit(solution)/shard_map/all_to_all | solution.py:359
  10.6 0.1 pad.6.clone
  10.7 3.6 %multipoles.1 = bf16[8,80,256]{2,1,0:T(8,128)(2,1)} custom-call(bf16[64,8192]{1,0:T(8,128)(2,1)} %density.1, bf16[64,8192]{1,0:T(8,128)(2,1)} %basis.1, bf16[32,4096]{1,0:T(8,128)(2,1)} %up_ref.1), custom_call_target="tpu_custom_call" | custom-call | tf_op jit(solution)/shard_map/multipoles/pallas_call | solution.py:398
  14.3 0.0 copy-start.5
  14.3 2.8 %all-to-all-done.1 = bf16[16,8,256]{2,1,0:T(8,128)(2,1)S(1)} async-done(((bf16[16,8,256]{2,1,0:T(8,128)(2,1)}), bf16[16,8,256]{2,1,0:T(8,128)(2,1)S(1)}, u32[]{:S(2)}, u32[]{:S(2)}) %all-to-all-start.1) | async-done | bytes 65568 | tf_op jit(solution)/shard_map/all_to_all | solution.py:359
  17.1 0.0 copy-done.10
  17.1 0.0 copy-done.3
  17.2 0.0 copy-done.8
  17.2 0.0 copy-start.7
  17.2 0.3 maximum_maximum_fusion.own
  17.5 0.0 copy-start.6
  17.5 3.6 %collective-permute-start.1 = (bf16[72,8192]{1,0:T(8,128)(2,1)S(1)}, bf16[72,8192]{1,0:T(8,128)(2,1)}, u32[]{:S(2)}, u32[]{:S(2)}) collective-permute-start(bf16[72,8192]{1,0:T(8,128)(2,1)S(1)} %maximum_maximum_fusion.own), channel_id=1, source_target_pairs={{1,2},{3,4},{5,6},{7,8},{9,10},{11,12},{13,14},{15,16},{17,18},{19... | collective-permute-start | bytes 3538952 | tf_op jit(solution)/shard_map/ppermute | solution.py:30
  21.0 0.0 collective-permute-start
  21.1 0.0 copy-done.5
  21.1 0.8 pad_maximum_fusion
  21.9 4.4 %all-to-all-start.2 = ((bf16[8,96,256]{2,1,0:T(8,128)(2,1)}), bf16[8,96,256]{2,1,0:T(8,128)(2,1)S(1)}, u32[]{:S(2)}, u32[]{:S(2)}) async-start(bf16[8,96,256]{2,1,0:T(8,128)(2,1)} %pad_maximum_fusion), calls=%async_computation.2 | async-start | bytes 786432 | tf_op jit(solution)/shard_map/all_to_all | solution.py:359
  26.3 0.7 pad_add_fusion.first
  26.9 2.0 %arrange.3 = bf16[8,128,256]{2,1,0:T(8,128)(2,1)} custom-call(bf16[8,8,4096]{2,1,0:T(8,128)(2,1)} %couple.1), custom_call_target="tpu_custom_call" | custom-call | tf_op jit(solution)/shard_map/arrange/pallas_call | solution.py:163
  29.0 0.0 copy-done.7
  29.0 0.5 reshape.7
  29.5 1.0 copy.18
  30.6 0.0 copy-done.6
  30.6 4.1 %arrange.2 = bf16[32,128,256]{2,1,0:T(8,128)(2,1)} custom-call(bf16[32,8,4096]{2,1,0:T(8,128)(2,1)} %couple), custom_call_target="tpu_custom_call" | custom-call | tf_op jit(solution)/shard_map/arrange/pallas_call | solution.py:163
  34.7 3.2 %all-to-all-done.2.refs_0_ = bf16[8,96,256]{2,1,0:T(8,128)(2,1)S(1)} async-done(((bf16[8,96,256]{2,1,0:T(8,128)(2,1)}), bf16[8,96,256]{2,1,0:T(8,128)(2,1)S(1)}, u32[]{:S(2)}, u32[]{:S(2)}) %all-to-all-start.2) | async-done | bytes 393248 | tf_op jit(solution)/shard_map/all_to_all | solution.py:359
  37.9 4.8 %serve.3 = bf16[128,56,256]{2,1,0:T(8,128)(2,1)} custom-call(bf16[8,96,256]{2,1,0:T(8,128)(2,1)S(1)} %all-to-all-done.2.refs_0_), custom_call_target="tpu_custom_call" | custom-call | tf_op jit(solution)/shard_map/serve/pallas_call | solution.py:139
  42.7 0.0 copy-done.4
  42.7 10.0 %all-to-all-start.3 = ((bf16[128,56,256]{2,1,0:T(8,128)(2,1)}), bf16[128,56,256]{2,1,0:T(8,128)(2,1)}, u32[]{:S(2)}, u32[]{:S(2)}) async-start(bf16[128,56,256]{2,1,0:T(8,128)(2,1)} %serve.3), calls=%async_computation.3 | async-start | bytes 7340032 | tf_op jit(solution)/shard_map/all_to_all | solution.py:359
  52.7 0.0 collective-permute-done.1.other_side
  52.7 0.0 collective-permute-done.one_side
  52.7 0.0 slice-start
  52.7 0.0 copy-start
  52.7 0.0 copy-start.1
  52.7 0.0 copy-start.2
  52.7 0.0 copy-start.9
  52.7 23.9 %near.1 = f32[32,64,256]{2,1,0:T(8,128)} custom-call(s32[9,32]{1,0:T(8,128)} %bitcast.16, s32[3]{0:T(128)} %pad_add_fusion.first, bf16[72,8192]{1,0:T(8,128)(2,1)} %collective-permute-done.one_side, bf16[72,8192]{1,0:T(8,128)(2,1)} %copy-done.6, bf16[72,8192]{1,0:T(8,128)(2,1)} %collective-permute-done.1.other_side), custom_call_target="tpu_custom_call" | custom-call | flops 483183820800 | bytes 6291456 | tf_op jit(solution)/shard_map/near/pallas_call | solution.py:236
  76.6 0.0 slice-done
  76.7 0.7 slice_reduce_fusion
  77.9 20.6 %all-to-all-done.3 = bf16[128,56,256]{2,1,0:T(8,128)(2,1)} async-done(((bf16[128,56,256]{2,1,0:T(8,128)(2,1)}), bf16[128,56,256]{2,1,0:T(8,128)(2,1)}, u32[]{:S(2)}, u32[]{:S(2)}) %all-to-all-start.3) | async-done | bytes 3670048 | tf_op jit(solution)/shard_map/all_to_all | solution.py:359
  98.5 0.0 copy-done
  98.5 0.0 copy-done.1
  98.5 0.0 copy-done.2
  98.5 0.0 copy-done.9
  98.5 6.6 %conditional.1 = (bf16[64,8192]{1,0:T(8,128)(2,1)}) conditional(s32[]{:T(128)} %convert_element_type.4, (s32[8,320]{1,0:T(8,128)S(1)}, bf16[128,56,256]{2,1,0:T(8,128)(2,1)}, bf16[8,128,256]{2,1,0:T(8,128)(2,1)S(1)}, bf16[8,256,64]{2,1,0:T(8,128)(2,1)S(1)}, bf16[32,128,256]{2,1,0:T(8,128)(2,1)S(1)}, /*index=5*/bf16[64,8192]{1,0:T(8,128)(2,1)}, ...), branch_computations={%region_1.2_spmd, %region_2.3_spmd} | conditional | bytes 3145736 | solution.py:450
  98.7 6.4 %far.2 = bf16[64,8192]{1,0:T(8,128)(2,1)} custom-call(s32[8,320]{1,0:T(8,128)S(1)} %get-tuple-element.38.refs_0_, bf16[128,56,256]{2,1,0:T(8,128)(2,1)} %get-tuple-element.39.refs_1_, bf16[8,128,256]{2,1,0:T(8,128)(2,1)S(1)} %get-tuple-element.40.refs_2_, bf16[8,256,64]{2,1,0:T(8,128)(2,1)S(1)} %get-tuple-element.41.refs_3_, ...), custom_call_target="tpu_custom_call" | custom-call | tf_op jit(solution)/shard_map/cond/branch_0_fun/far/pallas_call | solution.py:340
  (6 shorter events, 0.0 us)
Async XLA Ops:
  0.0 17.1 %copy-start.3 = (bf16[64,8192]{1,0:T(8,128)(2,1)S(1)}, bf16[64,8192]{1,0:T(8,128)(2,1)}, u32[]{:S(2)}) copy-start(bf16[64,8192]{1,0:T(8,128)(2,1)} %density.1) | copy-start | bytes 3145732
  0.0 17.1 %copy-start.10 = (bf16[8192]{0:T(1024)(128)(2,1)S(1)}, bf16[8192]{0:T(1024)(128)(2,1)}, u32[]{:S(2)}) copy-start(bf16[8192]{0:T(1024)(128)(2,1)} %param.18) | copy-start | bytes 49156
  0.0 17.2 %copy-start.8 = (bf16[3,8192]{1,0:T(4,128)(2,1)S(1)}, bf16[3,8192]{1,0:T(4,128)(2,1)}, u32[]{:S(2)}) copy-start(bf16[3,8192]{1,0:T(4,128)(2,1)} %param.17) | copy-start | bytes 147460
  2.0 15.1 %all-to-all-start.1 = ((bf16[16,8,256]{2,1,0:T(8,128)(2,1)}), bf16[16,8,256]{2,1,0:T(8,128)(2,1)S(1)}, u32[]{:S(2)}, u32[]{:S(2)}) async-start(bf16[16,8,256]{2,1,0:T(8,128)(2,1)} %get-tuple-element.72), calls=%async_computation.1 | async-start | bytes 131072 | tf_op jit(solution)/shard_map/all_to_all | solution.py:359
  14.3 6.8 %copy-start.5 = (bf16[8,80,256]{2,1,0:T(8,128)(2,1)S(1)}, bf16[8,80,256]{2,1,0:T(8,128)(2,1)}, u32[]{:S(2)}) copy-start(bf16[8,80,256]{2,1,0:T(8,128)(2,1)} %multipoles.1) | copy-start | bytes 983044
  17.2 11.8 %copy-start.7 = (bf16[32,4096]{1,0:T(8,128)(2,1)S(1)}, bf16[32,4096]{1,0:T(8,128)(2,1)}, u32[]{:S(2)}) copy-start(bf16[32,4096]{1,0:T(8,128)(2,1)} %param.22) | copy-start | bytes 786436
  17.5 13.1 %copy-start.6 = (bf16[72,8192]{1,0:T(8,128)(2,1)}, bf16[72,8192]{1,0:T(8,128)(2,1)S(1)}, u32[]{:S(2)}) copy-start(bf16[72,8192]{1,0:T(8,128)(2,1)S(1)} %maximum_maximum_fusion.own) | copy-start | bytes 3538948
  17.5 35.2 %collective-permute-start.1 = (bf16[72,8192]{1,0:T(8,128)(2,1)S(1)}, bf16[72,8192]{1,0:T(8,128)(2,1)}, u32[]{:S(2)}, u32[]{:S(2)}) collective-permute-start(bf16[72,8192]{1,0:T(8,128)(2,1)S(1)} %maximum_maximum_fusion.own), channel_id=1, source_target_pairs={{1,2},{3,4},{5,6},{7,8},{9,10},{11,12},{13,14},{15,16},{17,18},{19... | collective-permute-start | bytes 3538952 | tf_op jit(solution)/shard_map/ppermute | solution.py:30
  21.0 31.6 %collective-permute-start = (bf16[72,8192]{1,0:T(8,128)(2,1)S(1)}, bf16[72,8192]{1,0:T(8,128)(2,1)}, u32[]{:S(2)}, u32[]{:S(2)}) collective-permute-start(bf16[72,8192]{1,0:T(8,128)(2,1)S(1)} %maximum_maximum_fusion.own), channel_id=1, source_target_pairs={{0,1},{2,3},{4,5},{6,7},{8,9},{10,11},{12,13},{14,15},{16,17},{18,... | collective-permute-start | bytes 3538952 | tf_op jit(solution)/shard_map/ppermute | solution.py:30
  21.9 16.0 %all-to-all-start.2 = ((bf16[8,96,256]{2,1,0:T(8,128)(2,1)}), bf16[8,96,256]{2,1,0:T(8,128)(2,1)S(1)}, u32[]{:S(2)}, u32[]{:S(2)}) async-start(bf16[8,96,256]{2,1,0:T(8,128)(2,1)} %pad_maximum_fusion), calls=%async_computation.2 | async-start | bytes 786432 | tf_op jit(solution)/shard_map/all_to_all | solution.py:359
  37.9 4.8 %copy-start.4 = (bf16[8,96,256]{2,1,0:T(8,128)(2,1)}, bf16[8,96,256]{2,1,0:T(8,128)(2,1)S(1)}, u32[]{:S(2)}) copy-start(bf16[8,96,256]{2,1,0:T(8,128)(2,1)S(1)} %all-to-all-done.2.refs_0_) | copy-start | bytes 1179652
  42.7 55.8 %all-to-all-start.3 = ((bf16[128,56,256]{2,1,0:T(8,128)(2,1)}), bf16[128,56,256]{2,1,0:T(8,128)(2,1)}, u32[]{:S(2)}, u32[]{:S(2)}) async-start(bf16[128,56,256]{2,1,0:T(8,128)(2,1)} %serve.3), calls=%async_computation.3 | async-start | bytes 7340032 | tf_op jit(solution)/shard_map/all_to_all | solution.py:359
  52.7 24.0 %slice-start = ((bf16[8,96,256]{2,1,0:T(8,128)(2,1)}), bf16[8,16,256]{2,1,0:T(8,128)(2,1)S(1)}, s32[]{:S(2)}) async-start(bf16[8,96,256]{2,1,0:T(8,128)(2,1)} %copy-done.4), calls=%async_computation.4 | async-start | bytes 131072 | tf_op jit(solution)/shard_map/slice | solution.py:440
  52.7 45.8 %copy-start = (bf16[32,128,256]{2,1,0:T(8,128)(2,1)S(1)}, bf16[32,128,256]{2,1,0:T(8,128)(2,1)}, u32[]{:S(2)}) copy-start(bf16[32,128,256]{2,1,0:T(8,128)(2,1)} %arrange.2) | copy-start | bytes 6291460
  52.7 45.8 %copy-start.1 = (bf16[8,128,256]{2,1,0:T(8,128)(2,1)S(1)}, bf16[8,128,256]{2,1,0:T(8,128)(2,1)}, u32[]{:S(2)}) copy-start(bf16[8,128,256]{2,1,0:T(8,128)(2,1)} %arrange.3) | copy-start | bytes 1572868
  52.7 45.8 %copy-start.2 = (bf16[8,4,64,64]{2,3,1,0:T(8,128)(2,1)S(1)}, bf16[8,4,64,64]{2,3,1,0:T(8,128)(2,1)}, u32[]{:S(2)}) copy-start(bf16[8,4,64,64]{2,3,1,0:T(8,128)(2,1)} %copy.18) | copy-start | bytes 786436
  52.7 45.8 %copy-start.9 = (s32[8,320]{1,0:T(8,128)S(1)}, s32[8,320]{1,0:T(8,128)}, u32[]{:S(2)}) copy-start(s32[8,320]{1,0:T(8,128)} %get-tuple-element.86) | copy-start | bytes 30724
